TPU v7x, 128 devices: a whole 4x4x4 slice. The times are simulated.
128 devices in a mesh: dp: 4 (over y), ctx: 8 (over x, core), tensor: 4 (over z).
Axes of the slice: x: 4, y: 4, z: 4, core: 2. Of those that a mesh axis runs over, the one named last changes fastest.
Arguments:
- hidden_in: bfloat16 [4, 1536, 2048], P('dp', 'ctx'), may hold values from -6 to 6
- block_order: int32 [4, 16], P('dp'), may hold values from 0 to 15, each once within a row
- w_query: bfloat16 [2048, 2048], P(None, 'tensor'), may hold values from -0.125 to 0.125
- w_keyval: bfloat16 [2048, 512], P(None, 'tensor'), may hold values from -0.125 to 0.125
- w_output: bfloat16 [2048, 2048], P('tensor'), may hold values from -0.5 to 0.5
- w_gate: bfloat16 [2048, 5632], P(None, 'tensor'), may hold values from -0.125 to 0.125
- w_up: bfloat16 [2048, 5632], P(None, 'tensor'), may hold values from -0.125 to 0.125
- w_down: bfloat16 [5632, 2048], P('tensor'), may hold values from -0.078125 to 0.078125
- gain_attn: float32 [2048], replicated, may hold values from 0.5 to 1.5
- gain_ffn: float32 [2048], replicated, may hold values from 0.5 to 1.5
- cotangent: bfloat16 [4, 1536, 2048], P('dp', 'ctx'), may hold values from -6 to 6
Outputs:
- block_out: bfloat16 [4, 1536, 2048], P('dp', 'ctx')
- grad_input: float32 [4, 1536, 2048], P('dp', 'ctx')
- grad_query: float32 [2048, 2048], P(('dp', 'ctx'), 'tensor')
- grad_keyval: float32 [2048, 512], P(('dp', 'ctx'), 'tensor')
- grad_output: float32 [2048, 2048], P('tensor', ('dp', 'ctx'))
- grad_gate: float32 [2048, 5632], P(('dp', 'ctx'), 'tensor')
- grad_up: float32 [2048, 5632], P(('dp', 'ctx'), 'tensor')
- grad_down: float32 [5632, 2048], P('tensor', ('dp', 'ctx'))
- grad_gain_attn: float32 [2048], P(('dp', 'ctx'))
- grad_gain_ffn: float32 [2048], P(('dp', 'ctx'))
Inputs may be any that keep to these rules, and one draw needn't show every extreme that they name: `block_order`: each row names each of the 16 position blocks of its sequence exactly once.
All inputs are finite; a program needn't handle non-finite values.
Results may differ from a plain program's by a relative error of at most 0.03.
Values may be sent and summed in bfloat16 or wider, within the bound.
A program may use at most 128 MiB of HBM per device.

v0:
```python
import jax
import jax.numpy as jnp
from jax import lax
from jax.sharding import PartitionSpec as P

EPSILON = 1e-05
NEG_FILL = -1e30
ROPE_BASE = 10000.0


def shifted(x, axis, by):
    peers = lax.axis_size(axis)
    return lax.ppermute(x, axis, [(i, (i + by) % peers) for i in range(peers)])


def positions(order_row, first_row, row_count, block_rows):
    row_index = first_row + jnp.arange(row_count, dtype=jnp.int32)
    slot_index = row_index // block_rows
    slot_table = jnp.arange(order_row.shape[0], dtype=jnp.int32)
    chosen = jnp.sum(
        jnp.where(slot_index[:, None] == slot_table[None, :], order_row[None, :], 0), axis=1
    )
    return chosen * block_rows + row_index % block_rows


def angle_table(token_place, head_size):
    half_size = head_size // 2
    freq_table = ROPE_BASE ** (-jnp.arange(half_size, dtype=jnp.float32) / half_size)
    phases = token_place.astype(jnp.float32)[:, None] * freq_table[None, :]
    return (jnp.cos(phases), jnp.sin(phases))


def rotate(values, cosine_table, sine_table):
    half_size = values.shape[-1] // 2
    first_half = values[..., :half_size]
    second_half = values[..., half_size:]
    return jnp.concatenate(
        [
            first_half * cosine_table - second_half * sine_table,
            second_half * cosine_table + first_half * sine_table,
        ],
        -1,
    )


def per_device(
    hidden_in,
    block_order,
    w_query,
    w_keyval,
    w_output,
    w_gate,
    w_up,
    w_down,
    gain_attn,
    gain_ffn,
    cotangent,
):
    local_rows = hidden_in.shape[1]
    block_rows = local_rows // 2
    order_row = block_order[0]
    ctx_count = lax.axis_size("ctx")
    ctx_index = lax.axis_index("ctx")
    head_size = w_keyval.shape[1] // 2
    group_size = w_query.shape[1] // head_size
    score_scale = head_size ** (-0.5)
    own_place = positions(order_row, ctx_index * local_rows, local_rows, block_rows)
    cosine_table, sine_table = angle_table(own_place, head_size)
    residual = hidden_in[0].astype(jnp.float32)
    inv_first = lax.rsqrt(jnp.mean(residual * residual, -1, keepdims=True) + EPSILON)
    scaled_in = residual * inv_first
    normed = (scaled_in * gain_attn).astype(jnp.bfloat16)
    query_proj = jnp.dot(normed, w_query, preferred_element_type=jnp.float32)
    keyval_proj = jnp.dot(normed, w_keyval, preferred_element_type=jnp.float32)
    queries = rotate(
        query_proj.reshape(local_rows, group_size, head_size),
        cosine_table[:, None, :],
        sine_table[:, None, :],
    ).astype(jnp.bfloat16)
    key_rows = rotate(keyval_proj[:, :head_size], cosine_table, sine_table)
    keyval = jnp.concatenate([key_rows, keyval_proj[:, head_size:]], 1).astype(jnp.bfloat16)

    def masked_scores(key_piece, piece_start):
        key_place = positions(order_row, piece_start, key_piece.shape[0], block_rows)
        scores = (
            jnp.einsum(
                "qgd,kd->gqk", queries, key_piece[:, :head_size], preferred_element_type=jnp.float32
            )
            * score_scale
        )
        visible = key_place[None, None, :] <= own_place[None, :, None]
        return (scores, visible)

    key_piece = lax.all_gather(keyval, "ctx", axis=0, tiled=True)
    running_max = jnp.full((group_size, local_rows), NEG_FILL, jnp.float32)
    scores, visible = masked_scores(key_piece, jnp.int32(0))
    scores = jnp.where(visible, scores, NEG_FILL)
    new_max = jnp.maximum(running_max, jnp.max(scores, -1))
    probabilities = jnp.where(visible, jnp.exp(scores - new_max[..., None]), 0.0)
    running_sum = jnp.sum(probabilities, -1)
    weighted = jnp.einsum(
        "gqk,kd->gqd",
        probabilities.astype(jnp.bfloat16),
        key_piece[:, head_size:],
        preferred_element_type=jnp.float32,
    )
    final_max, final_sum, weighted = (new_max, running_sum, weighted)
    attended = weighted / final_sum[..., None]
    log_total = final_max + jnp.log(final_sum)
    attn_rows = (
        attended.transpose(1, 0, 2).reshape(local_rows, group_size * head_size).astype(jnp.bfloat16)
    )
    attn_out = lax.psum(
        jnp.dot(attn_rows, w_output, preferred_element_type=jnp.float32).astype(jnp.bfloat16),
        "tensor",
    ).astype(jnp.float32)
    mid_stream = residual + attn_out
    inv_second = lax.rsqrt(jnp.mean(mid_stream * mid_stream, -1, keepdims=True) + EPSILON)
    scaled_mid = mid_stream * inv_second
    normed_mid = (scaled_mid * gain_ffn).astype(jnp.bfloat16)
    gate_proj = jnp.dot(normed_mid, w_gate, preferred_element_type=jnp.float32)
    up_proj = jnp.dot(normed_mid, w_up, preferred_element_type=jnp.float32)
    gate_sig = jax.nn.sigmoid(gate_proj)
    activated = gate_proj * gate_sig
    inner_act = (activated * up_proj).astype(jnp.bfloat16)
    ffn_out = lax.psum(
        jnp.dot(inner_act, w_down, preferred_element_type=jnp.float32).astype(jnp.bfloat16),
        "tensor",
    ).astype(jnp.float32)
    result = (mid_stream + ffn_out).astype(jnp.bfloat16)
    seed_grad = cotangent[0]
    seed_wide = seed_grad.astype(jnp.float32)
    grad_down = jnp.einsum("tf,td->fd", inner_act, seed_grad, preferred_element_type=jnp.float32)
    grad_inner = jnp.einsum("td,fd->tf", seed_grad, w_down, preferred_element_type=jnp.float32)
    grad_gate_in = (grad_inner * up_proj * gate_sig * (1.0 + gate_proj * (1.0 - gate_sig))).astype(
        jnp.bfloat16
    )
    grad_up_in = (grad_inner * activated).astype(jnp.bfloat16)
    grad_gate = jnp.einsum(
        "td,tf->df", normed_mid, grad_gate_in, preferred_element_type=jnp.float32
    )
    grad_up = jnp.einsum("td,tf->df", normed_mid, grad_up_in, preferred_element_type=jnp.float32)
    mid_terms = jnp.einsum(
        "tf,df->td", grad_gate_in, w_gate, preferred_element_type=jnp.float32
    ) + jnp.einsum("tf,df->td", grad_up_in, w_up, preferred_element_type=jnp.float32)
    grad_normed_mid = lax.psum(mid_terms.astype(jnp.bfloat16), "tensor").astype(jnp.float32)
    grad_gain_ffn = jnp.sum(grad_normed_mid * scaled_mid, 0)
    scaled_grad = grad_normed_mid * gain_ffn
    grad_mid = seed_wide + inv_second * (
        scaled_grad - scaled_mid * jnp.mean(scaled_grad * scaled_mid, -1, keepdims=True)
    )
    grad_attn = grad_mid.astype(jnp.bfloat16)
    grad_output = jnp.einsum("tc,td->cd", attn_rows, grad_attn, preferred_element_type=jnp.float32)
    grad_rows = (
        jnp.einsum("td,cd->tc", grad_attn, w_output, preferred_element_type=jnp.float32)
        .astype(jnp.bfloat16)
        .reshape(local_rows, group_size, head_size)
    )
    row_delta = jnp.sum(grad_rows.astype(jnp.float32).transpose(1, 0, 2) * attended, -1)

    def piece_grads(key_piece, piece_start):
        scores, visible = masked_scores(key_piece, piece_start)
        probabilities = jnp.where(visible, jnp.exp(scores - log_total[..., None]), 0.0)
        probs_low = probabilities.astype(jnp.bfloat16)
        grad_values = jnp.einsum(
            "gqk,qgd->kd", probs_low, grad_rows, preferred_element_type=jnp.float32
        )
        grad_probs = jnp.einsum(
            "qgd,kd->gqk", grad_rows, key_piece[:, head_size:], preferred_element_type=jnp.float32
        )
        grad_scores = (probabilities * (grad_probs - row_delta[..., None])).astype(jnp.bfloat16)
        query_part = (
            jnp.einsum(
                "gqk,kd->qgd",
                grad_scores,
                key_piece[:, :head_size],
                preferred_element_type=jnp.float32,
            )
            * score_scale
        )
        grad_keys = (
            jnp.einsum("gqk,qgd->kd", grad_scores, queries, preferred_element_type=jnp.float32)
            * score_scale
        )
        return (query_part, jnp.concatenate([grad_keys, grad_values], 1))

    zero_queries = jnp.zeros((local_rows, group_size, head_size), jnp.float32)
    zero_keyval = jnp.zeros((local_rows, 2 * head_size), jnp.float32)

    def send_home(partial_sum):
        return shifted(partial_sum.astype(jnp.bfloat16), "ctx", 1).astype(partial_sum.dtype)

    def cycle_turn(turn_index, loop_state):
        grad_acc, current, partial_sum = loop_state
        source = (ctx_index - turn_index) % ctx_count
        query_part, keyval_part = piece_grads(current, source * local_rows)
        partial_sum = send_home(partial_sum + keyval_part)
        current = shifted(current, "ctx", 1)
        return (grad_acc + query_part, current, partial_sum)

    grad_queries, current, partial_sum = lax.fori_loop(
        0, ctx_count - 1, cycle_turn, (zero_queries, keyval, zero_keyval)
    )
    source = (ctx_index - (ctx_count - 1)) % ctx_count
    query_part, keyval_part = piece_grads(current, source * local_rows)
    grad_queries = grad_queries + query_part
    home_grads = send_home(partial_sum + keyval_part)
    grad_query_proj = (
        rotate(grad_queries, cosine_table[:, None, :], -sine_table[:, None, :])
        .reshape(local_rows, group_size * head_size)
        .astype(jnp.bfloat16)
    )
    grad_key_proj = rotate(home_grads[:, :head_size], cosine_table, -sine_table)
    grad_keyval_proj = jnp.concatenate([grad_key_proj, home_grads[:, head_size:]], 1).astype(
        jnp.bfloat16
    )
    grad_query = jnp.einsum(
        "td,tc->dc", normed, grad_query_proj, preferred_element_type=jnp.float32
    )
    grad_keyval = jnp.einsum(
        "td,tc->dc", normed, grad_keyval_proj, preferred_element_type=jnp.float32
    )
    in_terms = jnp.einsum(
        "tc,dc->td", grad_query_proj, w_query, preferred_element_type=jnp.float32
    ) + jnp.einsum("tc,dc->td", grad_keyval_proj, w_keyval, preferred_element_type=jnp.float32)
    grad_normed = lax.psum(in_terms.astype(jnp.bfloat16), "tensor").astype(jnp.float32)
    grad_gain_attn = jnp.sum(grad_normed * scaled_in, 0)
    scaled_back = grad_normed * gain_attn
    grad_input = grad_mid + inv_first * (
        scaled_back - scaled_in * jnp.mean(scaled_back * scaled_in, -1, keepdims=True)
    )
    (
        grad_query,
        grad_keyval,
        grad_output,
        grad_gate,
        grad_up,
        grad_down,
        grad_gain_attn,
        grad_gain_ffn,
    ) = (
        lax.psum_scatter(
            grad_query.astype(jnp.bfloat16), ("dp", "ctx"), scatter_dimension=0, tiled=True
        ).astype(jnp.float32),
        lax.psum_scatter(
            grad_keyval.astype(jnp.bfloat16), ("dp", "ctx"), scatter_dimension=0, tiled=True
        ).astype(jnp.float32),
        lax.psum_scatter(
            grad_output.astype(jnp.bfloat16), ("dp", "ctx"), scatter_dimension=1, tiled=True
        ).astype(jnp.float32),
        lax.psum_scatter(
            grad_gate.astype(jnp.bfloat16), ("dp", "ctx"), scatter_dimension=0, tiled=True
        ).astype(jnp.float32),
        lax.psum_scatter(
            grad_up.astype(jnp.bfloat16), ("dp", "ctx"), scatter_dimension=0, tiled=True
        ).astype(jnp.float32),
        lax.psum_scatter(
            grad_down.astype(jnp.bfloat16), ("dp", "ctx"), scatter_dimension=1, tiled=True
        ).astype(jnp.float32),
        lax.psum_scatter(
            grad_gain_attn.astype(jnp.bfloat16), ("dp", "ctx"), scatter_dimension=0, tiled=True
        ).astype(jnp.float32),
        lax.psum_scatter(
            grad_gain_ffn.astype(jnp.bfloat16), ("dp", "ctx"), scatter_dimension=0, tiled=True
        ).astype(jnp.float32),
    )
    return (
        result[None],
        grad_input[None],
        grad_query,
        grad_keyval,
        grad_output,
        grad_gate,
        grad_up,
        grad_down,
        grad_gain_attn,
        grad_gain_ffn,
    )


def solution(mesh):
    return jax.shard_map(
        per_device,
        mesh=mesh,
        in_specs=(
            P("dp", "ctx", None),
            P("dp", None),
            P(None, "tensor"),
            P(None, "tensor"),
            P("tensor", None),
            P(None, "tensor"),
            P(None, "tensor"),
            P("tensor", None),
            P(),
            P(),
            P("dp", "ctx", None),
        ),
        out_specs=(
            P("dp", "ctx", None),
            P("dp", "ctx", None),
            P(("dp", "ctx"), "tensor"),
            P(("dp", "ctx"), "tensor"),
            P("tensor", ("dp", "ctx")),
            P(("dp", "ctx"), "tensor"),
            P(("dp", "ctx"), "tensor"),
            P("tensor", ("dp", "ctx")),
            P(("dp", "ctx")),
            P(("dp", "ctx")),
        ),
        check_vma=False,
    )
```

profile of v0, /device:TPU:0, one launch (start us, length us, event | category | flops | bytes accessed | tf_op | source)
XLA Modules:
  0.0 822.9 jit_solution(9791609585317927842)
XLA Ops:
  9.2 1.7 fusion.74
  13.7 4.0 copy.96
  17.7 2.4 fusion.62
  20.1 1.6 copy.114
  22.4 1.6 multiply_cosine_fusion
  26.4 13.4 %all_gather.3 = bf16[1536,128]{1,0:T(8,128)(2,1)S(1)} all-gather(bf16[192,128]{1,0:T(8,128)(2,1)S(1)} %pad_maximum_fusion.2), channel_id=1, replica_groups=mesh['dp'=4,'ctx'=8,'tensor'=4] {'ctx'}, dimensions={0}, use_global_device_ids=true | all-gather | bytes 442368 | tf_op jit(solution)/shard_map/all_gather | solution.py:94
  41.6 1.8 fusion.18
  44.0 2.9 fusion.19
  47.0 3.5 fusion.67
  56.2 43.1 %all-reduce.8.cloned.1.call-done = bf16[192,2048]{1,0:T(8,128)(2,1)} async-done(((bf16[192,2048]{1,0:T(8,128)(2,1)}), bf16[192,2048]{1,0:T(8,128)(2,1)}) %all-reduce.8.cloned.1.call-update) | async-done | bytes 786448 | tf_op jit(solution)/shard_map/psum | solution.py:113
  99.3 1.5 multiply_reduce_fusion
  101.8 4.5 fusion.122
  108.2 3.1 multiply_convert_fusion.1
  111.4 2.0 fusion.124
  113.4 3.0 fusion.24
  116.7 1.7 pad_maximum_fusion
  119.8 5.1 convolution_convert_fusion.5
  124.9 37.0 %all-reduce.10.cloned.1.call-done = bf16[192,2048]{1,0:T(8,128)(2,1)} async-done(((bf16[192,2048]{1,0:T(8,128)(2,1)}), bf16[192,2048]{1,0:T(8,128)(2,1)}) %all-reduce.10.cloned.1.call-update) | async-done | bytes 786448 | tf_op jit(solution)/shard_map/psum | solution.py:146
  161.9 2.9 fusion.42
  165.4 1.7 convolution_convert_fusion.8
  169.3 77.9 %while.21 = (s32[]{:T(128)}, f32[192,8,64]{0,2,1:T(8,128)S(1)}, bf16[192,128]{0,1:T(8,128)(2,1)}, f32[192,128]{0,1:T(8,128)S(1)}, s32[]{:T(128)}, /*index=5*/s32...) while((s32[]{:T(128)}, f32[192,8,64]{0,2,1:T(8,128)S(1)}, ...), condition=%wide.region_13.14_spmd.clone, body=%wide.region_11.13_spmd.clone.sunk | while | flops 191287504 | bytes 9838325 | solution.py:201
  174.8 1.6 collective-permute-start.1
  176.7 3.0 collective-permute-done.1
  186.6 4.2 collective-permute-done.1
  197.4 4.6 collective-permute-done.1
  208.5 4.6 collective-permute-done.1
  219.6 4.6 collective-permute-done.1
  230.8 4.6 collective-permute-done.1
  241.9 4.6 collective-permute-done.1
  251.5 3.8 collective-permute-done.2
  260.1 3.4 convolution_convert_fusion.3
  264.2 2.2 convolution_convert_fusion.4
  267.7 4.3 convolution_convert_fusion.2
  273.0 4.3 convolution_convert_fusion.1
  278.4 4.3 convolution_convert_fusion
  284.7 47.7 %reduce-scatter.9.cloned.1.call-done = bf16[64,128]{1,0:T(8,128)(2,1)} async-done(((bf16[2048,128]{1,0:T(8,128)(2,1)}), bf16[64,128]{1,0:T(8,128)(2,1)}) %reduce-scatter.9.cloned.1.call-update) | async-done | bytes 16400 | tf_op jit(solution)/shard_map/reduce_scatter | solution.py:245
  333.7 51.9 %all-reduce.12.cloned.1.call-done = (bf16[192,2048]{1,0:T(8,128)(2,1)}, bf16[192,2048]{1,0:T(8,128)(2,1)}) async-done(((bf16[192,2048]{1,0:T(8,128)(2,1)}, bf16[192,2048]{1,0:T(8,128)(2,1)}), (bf16[192,2048]{1,0:T(8,128)(2,1)}, bf16[192,2048]{1,0:T(8,128)(2,1)})) %all-reduce.12.cloned.1.call-update) | async-done | bytes 1572880 | tf_op jit(solution)/shard_map/psum | solution.py:126
  385.6 1.8 fusion.45
  387.4 68.0 %all-reduce.2 = (bf16[2048]{0:T(1024)(128)(2,1)S(1)}, bf16[2048]{0:T(1024)(128)(2,1)S(1)}) all-reduce(bf16[2048]{0:T(1024)(128)(2,1)S(1)} %get-tuple-element.412, bf16[2048]{0:T(1024)(128)(2,1)S(1)} %copy-done.42), channel_id=8, replica_groups=mesh['dp'=4,'ctx'=8,'tensor'=4] {'dp','ctx'}, use_global_device_ids=true, to_apply=%region_24.25.clone | all-reduce | flops 4096 | bytes 16384
  456.5 4.9 fusion.38
  461.4 6.1 reduce-scatter.11.cloned.1.call-done
  469.0 80.0 %reduce-scatter.7.cloned.1.call-done = bf16[64,512]{1,0:T(8,128)(2,1)} async-done(((bf16[2048,512]{1,0:T(8,128)(2,1)}), bf16[64,512]{1,0:T(8,128)(2,1)}) %reduce-scatter.7.cloned.1.call-update) | async-done | bytes 65552 | tf_op jit(solution)/shard_map/reduce_scatter | solution.py:242
  550.6 86.9 %reduce-scatter.13.cloned.1.call-done = bf16[64,1408]{1,0:T(8,128)(2,1)} async-done(((bf16[2048,1408]{1,0:T(8,128)(2,1)}), bf16[64,1408]{1,0:T(8,128)(2,1)}) %reduce-scatter.13.cloned.1.call-update) | async-done | bytes 180240 | tf_op jit(solution)/shard_map/reduce_scatter | solution.py:251
  637.5 1.7 convert_element_type.243
  639.2 87.2 %reduce-scatter.15.cloned.1.call-done = bf16[64,1408]{1,0:T(8,128)(2,1)} async-done(((bf16[2048,1408]{1,0:T(8,128)(2,1)}), bf16[64,1408]{1,0:T(8,128)(2,1)}) %reduce-scatter.15.cloned.1.call-update) | async-done | bytes 180240 | tf_op jit(solution)/shard_map/reduce_scatter | solution.py:254
  726.3 1.7 convert_element_type.245
  728.0 86.7 %reduce-scatter.17.cloned.1.call-done = bf16[1408,64]{0,1:T(8,128)(2,1)} async-done(((bf16[1408,2048]{0,1:T(8,128)(2,1)}), bf16[1408,64]{0,1:T(8,128)(2,1)}) %reduce-scatter.17.cloned.1.call-update) | async-done | bytes 180240 | tf_op jit(solution)/shard_map/reduce_scatter | solution.py:257
  814.7 1.7 convert_element_type.247
  (310 shorter events, 88.0 us)
Async XLA Ops:
  7.2 44.0 %copy-start = (bf16[512,2048]{1,0:T(8,128)(2,1)S(1)}, bf16[512,2048]{1,0:T(8,128)(2,1)}, u32[]{:S(2)}) copy-start(bf16[512,2048]{1,0:T(8,128)(2,1)} %param.17) | copy-start | bytes 6291460
  7.2 92.1 %all-reduce.8.cloned.1.call-start = ((), (), s32[]{:S(2)}) async-start(), calls=%async_computation.6 | async-start | bytes 1572864 | tf_op jit(solution)/shard_map/psum | solution.py:113
  7.8 3.9 copy-start.35
  13.7 4.0 copy-start.2
  24.0 19.4 %copy-start.27 = (f32[192,32]{0,1:T(8,128)}, f32[192,32]{0,1:T(8,128)S(1)}, u32[]{:S(2)}) copy-start(f32[192,32]{0,1:T(8,128)S(1)} %get-tuple-element.460) | copy-start | bytes 73732
  52.7 48.7 %copy-start.32 = (f32[2048]{0:T(1024)S(1)}, f32[2048]{0:T(1024)}, u32[]{:S(2)}) copy-start(f32[2048]{0:T(1024)} %param.22) | copy-start | bytes 24580
  52.7 109.2 %all-reduce.10.cloned.1.call-start = ((), (), s32[]{:S(2)}) async-start(), calls=%async_computation.7 | async-start | bytes 1572864 | tf_op jit(solution)/shard_map/psum | solution.py:146
  101.4 4.9 slice-start
  101.7 4.6 copy-start.3
  101.8 4.6 slice-start.1
  101.8 6.0 slice-start.4
  106.4 5.0 slice-start.2
  108.2 3.1 slice-start.3
  116.4 216.0 %reduce-scatter.9.cloned.1.call-start = ((), (), s32[]{:S(2)}) async-start(), calls=%async_computation.9 | async-start | bytes 540672 | tf_op jit(solution)/shard_map/reduce_scatter | solution.py:245
  161.9 3.5 copy-start.6
  161.9 3.5 copy-start.13
  161.9 3.5 copy-start.15
  161.9 3.5 copy-start.40
  169.3 77.9 %copy-start.33 = (pred[192,192]{0,1:T(8,128)(4,1)S(1)}, pred[192,192]{0,1:T(8,128)(4,1)}, u32[]{:S(2)}) copy-start(pred[192,192]{0,1:T(8,128)(4,1)} %broadcast_compare_fusion.2) | copy-start | bytes 110596
  170.1 9.7 %collective-permute-start = (bf16[192,128]{0,1:T(8,128)(2,1)S(1)}, bf16[192,128]{0,1:T(8,128)(2,1)S(1)}, u32[]{:S(2)}, u32[]{:S(2)}) collective-permute-start(bf16[192,128]{0,1:T(8,128)(2,1)S(1)} %copy.124), channel_id=1, source_target_pairs={{0,4},{4,8},{8,12},{12,16},{16,20},{20,24},{24,28},{28,0},{1,5},{5... | collective-permute-start | bytes 147464 | tf_op jit(solution)/shard_map/while/body/eval_jaxpr/ppermute | solution.py:13
  174.8 4.9 collective-permute-start.1
  181.3 9.7 %collective-permute-start = (bf16[192,128]{0,1:T(8,128)(2,1)S(1)}, bf16[192,128]{0,1:T(8,128)(2,1)S(1)}, u32[]{:S(2)}, u32[]{:S(2)}) collective-permute-start(bf16[192,128]{0,1:T(8,128)(2,1)S(1)} %copy.124), channel_id=1, source_target_pairs={{0,4},{4,8},{8,12},{12,16},{16,20},{20,24},{24,28},{28,0},{1,5},{5... | collective-permute-start | bytes 147464 | tf_op jit(solution)/shard_map/while/body/eval_jaxpr/ppermute | solution.py:13
  186.0 4.9 collective-permute-start.1
  192.4 9.7 %collective-permute-start = (bf16[192,128]{0,1:T(8,128)(2,1)S(1)}, bf16[192,128]{0,1:T(8,128)(2,1)S(1)}, u32[]{:S(2)}, u32[]{:S(2)}) collective-permute-start(bf16[192,128]{0,1:T(8,128)(2,1)S(1)} %copy.124), channel_id=1, source_target_pairs={{0,4},{4,8},{8,12},{12,16},{16,20},{20,24},{24,28},{28,0},{1,5},{5... | collective-permute-start | bytes 147464 | tf_op jit(solution)/shard_map/while/body/eval_jaxpr/ppermute | solution.py:13
  197.1 4.9 collective-permute-start.1
  203.5 9.7 %collective-permute-start = (bf16[192,128]{0,1:T(8,128)(2,1)S(1)}, bf16[192,128]{0,1:T(8,128)(2,1)S(1)}, u32[]{:S(2)}, u32[]{:S(2)}) collective-permute-start(bf16[192,128]{0,1:T(8,128)(2,1)S(1)} %copy.124), channel_id=1, source_target_pairs={{0,4},{4,8},{8,12},{12,16},{16,20},{20,24},{24,28},{28,0},{1,5},{5... | collective-permute-start | bytes 147464 | tf_op jit(solution)/shard_map/while/body/eval_jaxpr/ppermute | solution.py:13
  208.2 4.9 collective-permute-start.1
  214.6 9.7 %collective-permute-start = (bf16[192,128]{0,1:T(8,128)(2,1)S(1)}, bf16[192,128]{0,1:T(8,128)(2,1)S(1)}, u32[]{:S(2)}, u32[]{:S(2)}) collective-permute-start(bf16[192,128]{0,1:T(8,128)(2,1)S(1)} %copy.124), channel_id=1, source_target_pairs={{0,4},{4,8},{8,12},{12,16},{16,20},{20,24},{24,28},{28,0},{1,5},{5... | collective-permute-start | bytes 147464 | tf_op jit(solution)/shard_map/while/body/eval_jaxpr/ppermute | solution.py:13
  219.3 4.9 collective-permute-start.1
  225.7 9.7 %collective-permute-start = (bf16[192,128]{0,1:T(8,128)(2,1)S(1)}, bf16[192,128]{0,1:T(8,128)(2,1)S(1)}, u32[]{:S(2)}, u32[]{:S(2)}) collective-permute-start(bf16[192,128]{0,1:T(8,128)(2,1)S(1)} %copy.124), channel_id=1, source_target_pairs={{0,4},{4,8},{8,12},{12,16},{16,20},{20,24},{24,28},{28,0},{1,5},{5... | collective-permute-start | bytes 147464 | tf_op jit(solution)/shard_map/while/body/eval_jaxpr/ppermute | solution.py:13
  230.5 4.9 collective-permute-start.1
  236.9 9.7 %collective-permute-start = (bf16[192,128]{0,1:T(8,128)(2,1)S(1)}, bf16[192,128]{0,1:T(8,128)(2,1)S(1)}, u32[]{:S(2)}, u32[]{:S(2)}) collective-permute-start(bf16[192,128]{0,1:T(8,128)(2,1)S(1)} %copy.124), channel_id=1, source_target_pairs={{0,4},{4,8},{8,12},{12,16},{16,20},{20,24},{24,28},{28,0},{1,5},{5... | collective-permute-start | bytes 147464 | tf_op jit(solution)/shard_map/while/body/eval_jaxpr/ppermute | solution.py:13
  241.6 4.9 collective-permute-start.1
  250.0 5.4 copy-start.43
  250.0 5.4 copy-start.46
  250.4 5.2 copy-start.31
  250.4 5.2 copy-start.37
  250.5 4.9 collective-permute-start.2
  251.5 5.6 copy-start.20
  251.5 5.6 copy-start.28
  257.1 128.5 %all-reduce.12.cloned.1.call-start = ((), (), s32[]{:S(2)}) async-start(), calls=%async_computation.14 | async-start | bytes 3145728 | tf_op jit(solution)/shard_map/psum | solution.py:126
  259.7 207.9 %reduce-scatter.11.cloned.1.call-start = ((), (), s32[]{:S(2)}) async-start(), calls=%async_computation.10 | async-start | bytes 2162688 | tf_op jit(solution)/shard_map/reduce_scatter | solution.py:248
  263.5 285.6 %reduce-scatter.7.cloned.1.call-start = ((), (), s32[]{:S(2)}) async-start(), calls=%async_computation.8 | async-start | bytes 2162688 | tf_op jit(solution)/shard_map/reduce_scatter | solution.py:242
  266.4 371.1 %reduce-scatter.13.cloned.1.call-start = ((), (), s32[]{:S(2)}) async-start(), calls=%async_computation.11 | async-start | bytes 5947392 | tf_op jit(solution)/shard_map/reduce_scatter | solution.py:251
  272.0 454.3 %reduce-scatter.15.cloned.1.call-start = ((), (), s32[]{:S(2)}) async-start(), calls=%async_computation.12 | async-start | bytes 5947392 | tf_op jit(solution)/shard_map/reduce_scatter | solution.py:254
  277.4 537.3 %reduce-scatter.17.cloned.1.call-start = ((), (), s32[]{:S(2)}) async-start(), calls=%async_computation.13 | async-start | bytes 5947392 | tf_op jit(solution)/shard_map/reduce_scatter | solution.py:257
  282.8 104.6 %copy-start.42 = (bf16[2048]{0:T(1024)(128)(2,1)S(1)}, bf16[2048]{0:T(1024)(128)(2,1)}, u32[]{:S(2)}) copy-start(bf16[2048]{0:T(1024)(128)(2,1)} %get-tuple-element.410) | copy-start | bytes 12292
  456.5 359.9 %copy-start.1 = (bf16[512,2048]{1,0:T(8,128)(2,1)S(1)}, bf16[512,2048]{1,0:T(8,128)(2,1)}, u32[]{:S(2)}) copy-start(bf16[512,2048]{1,0:T(8,128)(2,1)} %param.17) | copy-start | bytes 6291460
  (42 other events, 49.1 us)
Sparse Core Ops, SparseCore 0:
  52.8 46.4 all-reduce.7
  116.5 45.3 all-reduce.9
  257.2 75.1 reduce-scatter.8
  335.2 50.3 all-reduce.11
  389.0 78.5 reduce-scatter.10
  470.9 78.0 reduce-scatter.6
  552.8 84.5 reduce-scatter.12
  641.7 84.5 reduce-scatter.14
  730.1 84.5 reduce-scatter.16
where the time goes:
time: 825 us; the launch traced here: 823 us
  waiting for transfers between devices  561 us (68%)
  blocking collectives  81.4 us (10%)
  matrix products  77.5 us (9%)
  other arithmetic  51.3 us (6%)
  local copies, waits for them, and re-layouts  33.1 us (4%)
  between operations  15.1 us (2%)
    reduce_scatter x1, waiting for transfers between devices, per_device(): lax.psum_scatter(grad_up.astype(jnp.bfloat16), ('dp', 'ctx'), scatter_dim...  87.2 us
    reduce_scatter x1, waiting for transfers between devices, per_device(): lax.psum_scatter(grad_gate.astype(jnp.bfloat16), ('dp', 'ctx'), scatter_d...  86.9 us
    reduce_scatter x1, waiting for transfers between devices, per_device(): lax.psum_scatter(grad_down.astype(jnp.bfloat16), ('dp', 'ctx'), scatter_d...  86.7 us
    reduce_scatter x1, waiting for transfers between devices, per_device(): lax.psum_scatter(grad_query.astype(jnp.bfloat16), ('dp', 'ctx'), scatter_...  80 us
    unnamed x1, blocking collectives  68 us
    psum x1, waiting for transfers between devices, per_device(): lax.psum(jnp.dot(inner_act, w_down, preferred_element_type=jnp.float32).a...  51.9 us
    reduce_scatter x1, waiting for transfers between devices, per_device(): lax.psum_scatter(grad_keyval.astype(jnp.bfloat16), ('dp', 'ctx'), scatter...  47.7 us
    psum x1, waiting for transfers between devices, per_device(): lax.psum(jnp.dot(attn_rows, w_output, preferred_element_type=jnp.float32)...  43.1 us
  transfers between devices with their start and end apart: 24, of which 17 were waited for; matrix products, arithmetic and copies ran while one was open for 10% of the time, Pallas kernels for 0%

commit v1 on v0

v1 whole, which is shorter than its diff:
```python
import jax
import jax.numpy as jnp
import numpy as np
from jax import lax
from jax.experimental import pallas as pl
from jax.experimental.pallas import tpu as pltpu
from jax.sharding import PartitionSpec as P

MESH = pl.DeviceIdType.MESH
F32 = jnp.float32
BF16 = jnp.bfloat16
EPSILON = 1e-05
NEG_FILL = -1e30
ROPE_BASE = 10000.0

D = 2048
HD = 64
T = 192
BLOCK = 96
R = 48
QC = 512
FC = 1408
KEYS = 1536
PAIRS = 4
LANES = 384
GROUP = 384
FF_TILES = ((0, 384), (384, 384), (768, 384), (1152, 256))


def rope_tables():
    half = HD // 2
    freq = ROPE_BASE ** (-np.arange(half, dtype=np.float64) / half)
    freq = np.tile(freq, 4)[None, :]
    coarse = np.arange(16, dtype=np.float64)[:, None] * BLOCK * freq
    fine = np.arange(BLOCK, dtype=np.float64)[:, None] * freq
    coarse = np.stack([np.cos(coarse), np.sin(coarse)]).astype(np.float32)
    fine = np.stack([np.cos(fine), np.sin(fine)]).astype(np.float32)
    return coarse, fine


def dot(a, b):
    return jnp.dot(a, b, preferred_element_type=F32)


def dot_nt(a, b):
    return lax.dot_general(a, b, (((1,), (1,)), ((), ())), preferred_element_type=F32)


def tiles(total, size):
    return [(s, min(size, total - s)) for s in range(0, total, size)]


def lane_of(shape):
    return lax.broadcasted_iota(jnp.int32, shape, len(shape) - 1)


def swap_halves(t):
    first = lane_of(t.shape) % HD < HD // 2
    return jnp.where(first, pltpu.roll(t, 96, 1), pltpu.roll(t, 32, 1))


def layer_kernel(
    order, x_h, c_h, wq_h, wkv_h, wo_h, wg_h, wu_h, wd_h, ga, gf, coarse, fine,
    bo, gi, g_q, g_kv, g_o, g_g, g_u, g_d, gain_a, gain_f,
    x, cot, wq, wkv, wo, wg, wu, wd, row_g, row_u, row_q, row_kv,
    xn, kvall, kk, vv, kt, vt, qst, cos_t, sin_t, s_buf, pt, ob, rl,
    zs, zr, mid, dmid, hn, da, dinner, act, act_p,
    xn_t, c_t, hn_t, xn_p, c_p, hn_p, da_p, ob_p, dqp, dqp_p, dkvp, dkvp_p,
    dkv_r, delta,
    r1f, r2f, r3f, r4f, r1a, r2a, r3a, r4a, gain_s, gain_r,
    load_sem, send_sem, recv_sem,
):
    iy = lax.axis_index("dp")
    ictx = lax.axis_index("ctx")
    iz = lax.axis_index("tensor")
    ix = ictx // 2
    core = ictx % 2
    other = 1 - core

    def z_peer(k):
        return (iy, ictx, (iz + k) % 4)

    def ctx_peer(k):
        return (iy, (ictx + k) % 8, iz)

    def x_peer(k):
        return (iy, ((ix + k) % 4) * 2 + core, iz)

    def y_peer(k):
        return ((iy + k) % 4, ictx, iz)

    core_peer = (iy, ix * 2 + other, iz)

    loads = {}

    def load(name, src, dst):
        copy = pltpu.make_async_copy(src, dst, load_sem.at[len(loads)])
        copy.start()
        loads[name] = copy

    load("x", x_h, x)
    load("wkv", wkv_h, wkv)
    load("wq", wq_h, wq)
    load("cot", c_h, cot)
    load("wd", wd_h, wd)
    load("wo", wo_h, wo)
    load("wg", wg_h, wg)
    load("wu", wu_h, wu)
    own_h, own_a, own_b = iy // 2, (iy % 2) * 2 + ix // 2, (ix % 2) * 2 + core
    load("row_g", wg_h.at[own_h, own_a, own_b], row_g)
    load("row_u", wu_h.at[own_h, own_a, own_b], row_u)
    own_rows = pl.ds(pl.multiple_of(((iy * 4 + ix) * 2 + core) * 64, 64), 64)
    load("row_q", wq_h.at[own_rows], row_q)
    load("row_kv", wkv_h.at[own_rows], row_kv)

    barrier = pltpu.get_barrier_semaphore()
    greeted = (
        [ctx_peer(k) for k in range(1, 8)]
        + [z_peer(k) for k in range(1, 4)]
        + [y_peer(1), y_peer(3)]
    )
    for peer in greeted:
        pl.semaphore_signal(barrier, inc=1, device_id=peer, device_id_type=MESH)
    pl.semaphore_wait(barrier, len(greeted))

    sent = []

    def send(src, dst, peer):
        n = len(sent)
        copy = pltpu.make_async_remote_copy(
            src_ref=src, dst_ref=dst, send_sem=send_sem.at[n], recv_sem=recv_sem.at[n],
            device_id=peer, device_id_type=MESH,
        )
        copy.start()
        sent.append(copy)
        return copy

    def wait_recv(copies):
        for copy in copies:
            copy.wait_recv()

    released = set()

    def wait_send(copies):
        for copy in copies:
            copy.wait_send()
            released.add(id(copy))

    pick = lax.broadcasted_iota(jnp.int32, (16, 128), 0)
    sign = jnp.where(lane_of((BLOCK, 128)) % HD < HD // 2, -1.0, 1.0).astype(F32)
    for b in range(2):
        chosen = pick == order[0, ictx * 2 + b]
        ca = jnp.sum(jnp.where(chosen, coarse[0], 0.0), 0, keepdims=True)
        sa = jnp.sum(jnp.where(chosen, coarse[1], 0.0), 0, keepdims=True)
        cos_t[b * BLOCK : (b + 1) * BLOCK, :] = ca * fine[0] - sa * fine[1]
        sin_t[b * BLOCK : (b + 1) * BLOCK, :] = (sa * fine[0] + ca * fine[1]) * sign

    def rot(t):
        return t * cos_t[...] + swap_halves(t) * sin_t[...]

    def rot_back(t):
        return t * cos_t[...] - swap_halves(t) * sin_t[...]

    def inv_rms(v):
        return lax.rsqrt(jnp.mean(v * v, -1, keepdims=True) + EPSILON)

    low_lane = lane_of((T, 128)) < HD

    loads["x"].wait()
    for i in range(4):
        rows = x[i].astype(F32)
        xn[i] = (rows * inv_rms(rows) * ga[...]).astype(BF16)
    loads["wkv"].wait()
    normed = xn[...].reshape(T, D)
    kvp = dot(normed, wkv[...])
    kvall[ictx] = jnp.where(low_lane, rot(kvp), kvp).astype(BF16)
    kv_copies = [send(kvall.at[ictx], kvall.at[ictx], ctx_peer(k)) for k in range(1, 8)]

    loads["wq"].wait()
    for s, n in tiles(QC, 256):
        qp = dot(normed, wq[:, s : s + n])
        for j in range(n // 128):
            p = s // 128 + j
            q = rot(qp[:, j * 128 : (j + 1) * 128]) * (HD ** -0.5)
            qst[p, 0:T, :] = jnp.where(low_lane, q, 0.0).astype(BF16)
            qst[p, T : 2 * T, :] = jnp.where(low_lane, 0.0, q).astype(BF16)

    xn_t[...] = normed.T.reshape(16, 2, 64, T)
    xnt_copy = send(xn_t.at[:, other], xn_p, core_peer)
    loads["cot"].wait()
    cot_rows = cot[...].reshape(T, D)
    c_t[...] = cot_rows.T.reshape(16, 2, 64, T)
    ct_copy = send(c_t.at[:, other], c_p, core_peer)
    loads["wd"].wait()
    for s, n in tiles(FC, 256):
        dinner[:, s : s + n] = dot_nt(cot_rows, wd[s : s + n, :])

    wait_recv(kv_copies)
    for j in range(8):
        t = kvall[j]
        wide = t.astype(F32)
        turned = pltpu.roll(wide, HD, 1)
        rows = pl.ds(j * T, T)
        kk[rows, :] = jnp.where(low_lane, wide, turned).astype(BF16)
        vv[rows, :] = jnp.where(low_lane, turned, wide).astype(BF16)
    kv_t = kvall[...].reshape(KEYS, 128).T
    kt[0:HD, :] = kv_t[0:HD]
    kt[HD : 2 * HD, :] = kv_t[0:HD]
    vt[0:HD, :] = kv_t[HD : 2 * HD]
    vt[HD : 2 * HD, :] = kv_t[HD : 2 * HD]
    vt[2 * HD : 2 * HD + 16, :] = jnp.ones((16, KEYS), BF16)

    token = lane_of((1, LANES))
    token = jnp.where(token >= T, token - T, token)
    q_place = jnp.where(
        token >= BLOCK,
        order[0, ictx * 2 + 1] * BLOCK + token - BLOCK,
        order[0, ictx * 2] * BLOCK + token,
    )
    key_row = lax.broadcasted_iota(jnp.int32, (BLOCK, LANES), 0)
    n_groups = KEYS // GROUP

    for p in range(PAIRS):

        def score_group(i, top):
            r0 = pl.multiple_of(i * GROUP, GROUP)
            scores = dot_nt(kk[pl.ds(r0, GROUP), :], qst[p])
            parts = []
            for b in range(GROUP // BLOCK):
                limit = q_place - order[0, i * (GROUP // BLOCK) + b] * BLOCK
                parts.append(
                    jnp.where(key_row <= limit, scores[b * BLOCK : (b + 1) * BLOCK], NEG_FILL)
                )
            scores = jnp.concatenate(parts, 0)
            s_buf[pl.ds(r0, GROUP), :] = scores
            return jnp.maximum(top, jnp.max(scores, 0, keepdims=True))

        top = lax.fori_loop(0, n_groups, score_group, jnp.full((1, LANES), NEG_FILL, F32))

        def weight_group(i, carry):
            r0 = pl.multiple_of(i * GROUP, GROUP)
            pt[p, pl.ds(r0, GROUP), :] = jnp.exp(s_buf[pl.ds(r0, GROUP), :] - top).astype(BF16)
            return carry

        lax.fori_loop(0, n_groups, weight_group, 0)
        summed = dot(vt[...], pt[p])
        inv = 1.0 / summed[2 * HD : 2 * HD + 1]
        out = summed[0 : 2 * HD] * inv
        pair = slice(p * 128, (p + 1) * 128)
        ob[:, pair] = jnp.where(low_lane, out[:, 0:T].T, out[:, T : 2 * T].T).astype(BF16)
        inv_wide = jnp.broadcast_to(inv, (2 * HD, LANES))
        rl[:, pair] = jnp.where(low_lane, inv_wide[:, 0:T].T, inv_wide[:, T : 2 * T].T)

    ob_copy = send(ob, ob_p, core_peer)

    def z_scatter(slot, n):
        return [
            send(slot.at[(iz + k) % 4], zr.at[n, k - 1], z_peer(k)) for k in range(1, 4)
        ]

    def z_sum(slot, n):
        total = slot[iz].astype(F32)
        for k in range(3):
            total = total + zr[n, k].astype(F32)
        return total

    def z_gather(buf):
        return [send(buf.at[iz], buf.at[iz], z_peer(k)) for k in range(1, 4)]

    loads["wo"].wait()
    rows_o = ob[...]
    for s, n in tiles(D, 512):
        zs[:, :, s : s + n] = dot(rows_o, wo[:, s : s + n]).astype(BF16).reshape(4, R, n)
    attn_copies = z_scatter(zs, 0)
    wait_recv(attn_copies)
    mid[...] = x[iz].astype(F32) + z_sum(zs, 0)
    m = mid[...]
    hn[iz] = (m * inv_rms(m) * gf[...]).astype(BF16)
    hn_copies = z_gather(hn)

    loads["wg"].wait()
    loads["wu"].wait()
    wait_recv(hn_copies)
    hidden = hn[...].reshape(T, D)
    for s, n in FF_TILES:
        cols = slice(s, s + n)
        g = dot(hidden, wg[:, :, :, :, :, cols].reshape(D, n))
        u = dot(hidden, wu[:, :, :, :, :, cols].reshape(D, n))
        sig = 1.0 / (1.0 + jnp.exp(-g))
        a = g * sig
        di = dinner[:, cols]
        act[0, :, cols] = (a * u).astype(BF16)
        act[1, :, cols] = (di * u * sig * (1.0 + g * (1.0 - sig))).astype(BF16)
        act[2, :, cols] = (di * a).astype(BF16)
    act_copies = [send(act.at[i], act_p.at[i], core_peer) for i in range(3)]

    wait_send(attn_copies)

    def dhn_tile(t, carry):
        r = dot_nt(act[1], wg[t // 4, t % 4].reshape(256, FC))
        r = r + dot_nt(act[2], wu[t // 4, t % 4].reshape(256, FC))
        zs[:, :, pl.ds(pl.multiple_of(t * 256, 256), 256)] = r.astype(BF16).reshape(4, R, 256)
        return carry

    lax.fori_loop(0, 8, dhn_tile, 0)
    dhn_copies = z_scatter(zs, 1)

    hn_t[...] = hidden.T.reshape(16, 2, 64, T)
    hnt_copy = send(hn_t.at[:, other], hn_p, core_peer)
    inner = act[0]
    for s, n in tiles(D, 512):
        xn[:, :, s : s + n] = dot(inner, wd[:, s : s + n]).astype(BF16).reshape(4, R, n)

    def weight_grad(own_t, partner_t, own_b, partner_b, ref, half, c0, n):
        a_own = own_t[:, core].reshape(1024, T)
        a_partner = partner_t[...].reshape(1024, T)
        for s, w in tiles(n, 256):
            r = dot(a_own, own_b[:, s : s + w]) + dot(a_partner, partner_b[:, s : s + w])
            ref[half, :, :, :, :, c0 + s : c0 + s + w] = r.astype(BF16).reshape(4, 4, 2, 32, w)

    xp, xm, x2 = (ix + 1) % 4, (ix + 3) % 4, (ix + 2) % 4
    yp, ym, y2 = (iy + 1) % 4, (iy + 3) % 4, (iy + 2) % 4
    f_bufs = [[r.at[i] for r in (r1f, r2f, r3f, r4f)] for i in range(3)]
    a_bufs = [r1a, r2a, r3a, r4a]
    parts = [
        (wg, 1, 0, FC, f_bufs[0], 0),
        (wg, 0, 0, FC, f_bufs[1], 0),
        (wu, 0, 0, FC, f_bufs[2], 0),
        (wu, 1, 0, 512, a_bufs, 0),
        (wu, 1, 512, 640, a_bufs, 512),
    ]
    flights = {}
    lo2, hi2, all4 = pl.ds(0, 2), pl.ds(2, 2), pl.ds(0, 4)
    all32, lo16, hi16 = pl.ds(0, 32), pl.ds(0, 16), pl.ds(16, 16)

    def g_index(part, dy, dx, h, rows=None):
        ref, half, c0, n, _, _ = parts[part]
        return (half, dy, dx, h, all32 if rows is None else rows, pl.ds(c0, n))

    def outgoing(part, step):
        if step == 0:
            return (
                (g_index(part, lo2, x2, 0), g_index(part, hi2, x2, 0)),
                (g_index(part, y2, lo2, 1), g_index(part, y2, hi2, 1)),
            )
        if step == 1:
            return (
                (g_index(part, all4, xp, 0), g_index(part, all4, xm, 0)),
                (g_index(part, yp, all4, 1), g_index(part, ym, all4, 1)),
            )
        if step == 2:
            return (
                (g_index(part, y2, ix, 0, lo16), g_index(part, y2, ix, 0, hi16)),
                (g_index(part, iy, x2, 1, lo16), g_index(part, iy, x2, 1, hi16)),
            )
        return (
            (g_index(part, yp, ix, 0), g_index(part, ym, ix, 0)),
            (g_index(part, iy, xp, 1), g_index(part, iy, xm, 1)),
        )

    def landing(part, step, flow, way):
        _, _, _, n, bufs, b0 = parts[part]
        return bufs[step].at[flow, way, ..., pl.ds(b0, n)]

    def rs_send(part, step):
        ref = parts[part][0]
        out = outgoing(part, step)
        for flow in range(2):
            along_x = (flow == 0) == (step < 2)
            for way, k in ((0, 1), (1, 3)):
                peer = x_peer(k) if along_x else y_peer(k)
                flights[part, step, flow, way] = send(
                    ref.at[out[flow][way]], landing(part, step, flow, way), peer
                )

    def add_in(ref, index, *arrived):
        total = ref[index].astype(F32)
        for a in arrived:
            total = total + a[...].astype(F32)
        ref[index] = total.astype(BF16)

    def rs_recv(part, step):
        ref = parts[part][0]
        for flow in range(2):
            wait_recv([flights[part, step, flow, way] for way in range(2)])
            got = [landing(part, step, flow, way) for way in range(2)]
            if step == 0:
                if flow == 0:
                    add_in(ref, g_index(part, lo2, xp, 0), got[0])
                    add_in(ref, g_index(part, hi2, xm, 0), got[1])
                else:
                    add_in(ref, g_index(part, yp, lo2, 1), got[0])
                    add_in(ref, g_index(part, ym, hi2, 1), got[1])
            elif step == 1:
                if flow == 0:
                    add_in(ref, g_index(part, all4, ix, 0), *got)
                else:
                    add_in(ref, g_index(part, iy, all4, 1), *got)
            elif step == 2:
                if flow == 0:
                    add_in(ref, g_index(part, yp, ix, 0, lo16), got[0])
                    add_in(ref, g_index(part, ym, ix, 0, hi16), got[1])
                else:
                    add_in(ref, g_index(part, iy, xp, 1, lo16), got[0])
                    add_in(ref, g_index(part, iy, xm, 1, hi16), got[1])

    def rs_turn(part, step):
        rs_recv(part, step)
        rs_send(part, step + 1)

    def rs_last(part, outs):
        rs_recv(part, 3)
        ref = parts[part][0]
        for flow in range(2):
            total = ref[g_index(part, iy, ix, flow)].astype(F32)
            for way in range(2):
                total = total + landing(part, 3, flow, way)[...].astype(F32)
            for out, s, n in outs:
                out[flow * 32 : (flow + 1) * 32, :] = total[:, s : s + n]

    wait_recv([ct_copy, act_copies[0]])
    weight_grad(c_t, c_p, act.at[0], act_p.at[0], wg, 1, 0, FC)
    rs_send(0, 0)
    wait_recv([hnt_copy, act_copies[1]])
    weight_grad(hn_t, hn_p, act.at[1], act_p.at[1], wg, 0, 0, FC)
    rs_send(1, 0)
    wait_recv([act_copies[2]])
    weight_grad(hn_t, hn_p, act.at[2], act_p.at[2], wu, 0, 0, FC)
    rs_send(2, 0)

    wait_recv(dhn_copies)
    m = mid[...]
    r2 = inv_rms(m)
    mhat = m * r2
    scaled = z_sum(zs, 1) * gf[...]
    dm = cot[iz].astype(F32) + r2 * (
        scaled - mhat * jnp.mean(scaled * mhat, -1, keepdims=True)
    )
    dmid[...] = dm
    da[iz] = dm.astype(BF16)
    da_copies = z_gather(da)
    ffn_copies = z_scatter(xn, 2)

    rs_turn(0, 0)
    rs_turn(1, 0)
    rs_turn(2, 0)

    wait_recv(da_copies)
    grad_attn = da[...].reshape(T, D)
    for s, n in tiles(QC, 256):
        grad_rows = dot_nt(grad_attn, wo[s : s + n, :])
        for j in range(n // 128):
            p = s // 128 + j
            pair = slice(p * 128, (p + 1) * 128)
            g = grad_rows[:, j * 128 : (j + 1) * 128] * rl[:, pair]
            dob = kk.at[p * LANES : (p + 1) * LANES]
            dob[0:T, :] = jnp.where(low_lane, g, 0.0).astype(BF16)
            dob[T : 2 * T, :] = jnp.where(low_lane, 0.0, g).astype(BF16)
            by_row = (g * ob[:, pair].astype(F32)).T
            delta[p] = jnp.concatenate(
                [
                    jnp.sum(by_row[0:HD], 0, keepdims=True),
                    jnp.sum(by_row[HD : 2 * HD], 0, keepdims=True),
                ],
                1,
            )
    wait_send([ct_copy])
    c_t[...] = grad_attn.T.reshape(16, 2, 64, T)
    dat_copy = send(c_t.at[:, other], da_p, core_peer)

    wait_send(kv_copies)
    for p in range(PAIRS):
        dob = kk.at[p * LANES : (p + 1) * LANES]

        def grad_group(i, carry):
            r0 = pl.multiple_of(i * GROUP, GROUP)
            rows = pl.ds(r0, GROUP)
            weights = pt[p, rows, :]
            grad_weights = dot_nt(vv[rows, :], dob[...])
            grad_scores = (weights.astype(F32) * (grad_weights - delta[p])).astype(BF16)
            pt[p, rows, :] = grad_scores
            dv = dot(weights, dob[...])
            dk = dot(grad_scores, qst[p])
            if p > 0:
                dk = dk + s_buf[rows, 0:128]
                dv = dv + s_buf[rows, 128:256]
            s_buf[rows, 0:128] = dk
            s_buf[rows, 128:256] = dv
            return carry

        lax.fori_loop(0, n_groups, grad_group, 0)
        dq = dot(kt[...], pt[p]) * (HD ** -0.5)
        dq = jnp.where(low_lane, dq[:, 0:T].T, dq[:, T : 2 * T].T)
        dqp[:, p * 128 : (p + 1) * 128] = rot_back(dq).astype(BF16)

    for j in range(8):
        rows = slice(j * T, (j + 1) * T)
        dk, dv = s_buf[rows, 0:128], s_buf[rows, 128:256]
        kvall[j] = jnp.where(
            low_lane, dk + pltpu.roll(dk, HD, 1), dv + pltpu.roll(dv, HD, 1)
        ).astype(BF16)
    dkv_copies = [
        send(kvall.at[(ictx + k) % 8], dkv_r.at[k - 1], ctx_peer(k)) for k in range(1, 8)
    ]
    dqp_copy = send(dqp, dqp_p, core_peer)

    wait_recv(ffn_copies)
    bo[iz] = (mid[...] + z_sum(xn, 2)).astype(BF16)
    bo_copies = z_gather(bo)

    wait_recv([dat_copy, ob_copy])
    weight_grad(c_t, da_p, ob, ob_p, wu, 1, 0, 512)
    rs_send(3, 0)
    rs_turn(0, 1)

    wait_recv(dkv_copies)
    home = kvall[ictx].astype(F32)
    for k in range(7):
        home = home + dkv_r[k].astype(F32)
    dkvp[...] = jnp.where(low_lane, rot_back(home), home).astype(BF16)
    dkvp_copy = send(dkvp, dkvp_p, core_peer)
    wait_send(dhn_copies)
    q_rows, kv_rows = dqp[...], dkvp[...]
    for s, n in tiles(D, 512):
        r = dot_nt(q_rows, wq[s : s + n, :]) + dot_nt(kv_rows, wkv[s : s + n, :])
        zs[:, :, s : s + n] = r.astype(BF16).reshape(4, R, n)
    dxn_copies = z_scatter(zs, 3)

    wait_recv([xnt_copy, dqp_copy])
    weight_grad(xn_t, xn_p, dqp, dqp_p, wu, 1, 512, 512)
    wait_recv([dkvp_copy])
    weight_grad(xn_t, xn_p, dkvp, dkvp_p, wu, 1, 1024, 128)
    rs_send(4, 0)
    rs_turn(1, 1)

    wait_recv(dxn_copies)
    rows = x[iz].astype(F32)
    r1 = inv_rms(rows)
    xhat = rows * r1
    scaled = z_sum(zs, 3) * ga[...]
    gi[iz] = (
        dmid[...] + r1 * (scaled - xhat * jnp.mean(scaled * xhat, -1, keepdims=True))
    ).astype(BF16)
    gi_copies = z_gather(gi)

    rs_turn(2, 1)
    rs_turn(3, 0)
    rs_turn(4, 0)
    rs_turn(0, 2)
    rs_turn(1, 2)
    rs_turn(2, 2)
    rs_turn(3, 1)
    rs_turn(4, 1)
    rs_turn(3, 2)
    rs_turn(4, 2)
    rs_last(0, [(g_d, 0, FC)])
    rs_last(1, [(g_g, 0, FC)])
    rs_last(2, [(g_u, 0, FC)])
    rs_last(3, [(g_o, 0, 512)])
    rs_last(4, [(g_q, 0, 512), (g_kv, 512, 128)])

    for name in ("row_g", "row_u", "row_q", "row_kv"):
        loads[name].wait()

    def row_products(pairs):
        total = jnp.zeros((64, 128), F32)
        for grad, weight in pairs:
            n = grad.shape[-1]
            w = weight[...].reshape(64, n)
            for s, _ in tiles(n, 128):
                total = total + grad[:, s : s + 128] * w[:, s : s + 128].astype(F32)
        return jnp.sum(total.T, 0, keepdims=True)

    gain_s[...] = jnp.zeros((8, 128), F32)
    gain_s[0:1, 0:64] = row_products([(g_g, row_g), (g_u, row_u)])
    gain_s[1:2, 0:64] = row_products([(g_q, row_q), (g_kv, row_kv)])
    gain_copies = [send(gain_s, gain_r.at[k - 1], z_peer(k)) for k in range(1, 4)]
    wait_recv(gain_copies)
    total = gain_s[...]
    for k in range(3):
        total = total + gain_r[k]
    chip_cols = pl.ds(pl.multiple_of((iy * 4 + ix) * 128, 128), 128)

    def own_gain(ref):
        v = ref[:, chip_cols]
        return jnp.where(core == 1, pltpu.roll(v, 64, 1), v)[:, 0:64]

    gain_f[...] = total[0:1, 0:64] / own_gain(gf)
    gain_a[...] = total[1:2, 0:64] / own_gain(ga)

    wait_recv(bo_copies)
    wait_recv(gi_copies)
    wait_send([copy for copy in sent if id(copy) not in released])


N_SENDS = 131


def per_device(
    hidden_in, block_order, w_query, w_keyval, w_output, w_gate, w_up, w_down,
    gain_attn, gain_ffn, cotangent,
):
    coarse, fine = rope_tables()
    any_spec = pl.BlockSpec(memory_space=pl.ANY)
    vmem = pl.BlockSpec(memory_space=pltpu.VMEM)
    smem = pl.BlockSpec(memory_space=pltpu.SMEM)
    shape = jax.ShapeDtypeStruct
    wide = (2, 4, 4, 2, 32, FC)
    turned = (16, 2, 64, T)
    half_turned = (16, 64, T)
    scratch = [
        pltpu.VMEM(s, t)
        for s, t in (
            ((4, R, D), BF16), ((4, R, D), BF16),
            ((D, QC), BF16), ((D, 128), BF16), ((QC, D), BF16),
            (wide, BF16), (wide, BF16), ((FC, D), BF16),
            ((2, 32, FC), BF16), ((2, 32, FC), BF16), ((64, QC), BF16), ((64, 128), BF16),
            ((4, R, D), BF16), ((8, T, 128), BF16),
            ((KEYS, 128), BF16), ((KEYS, 128), BF16),
            ((128, KEYS), BF16), ((144, KEYS), BF16),
            ((PAIRS, LANES, 128), BF16), ((T, 128), F32), ((T, 128), F32),
            ((KEYS, LANES), F32), ((PAIRS, KEYS, LANES), BF16),
            ((T, QC), BF16), ((T, QC), F32),
            ((4, R, D), BF16), ((4, 3, R, D), BF16),
            ((R, D), F32), ((R, D), F32),
            ((4, R, D), BF16), ((4, R, D), BF16), ((T, FC), F32),
            ((3, T, FC), BF16), ((3, T, FC), BF16),
            (turned, BF16), (turned, BF16), (turned, BF16),
            (half_turned, BF16), (half_turned, BF16), (half_turned, BF16), (half_turned, BF16),
            ((T, QC), BF16), ((T, QC), BF16), ((T, QC), BF16),
            ((T, 128), BF16), ((T, 128), BF16),
            ((7, T, 128), BF16),
            ((PAIRS, 1, LANES), F32),
            ((3, 2, 2, 2, 32, FC), BF16), ((3, 2, 2, 4, 32, FC), BF16),
            ((3, 2, 2, 16, FC), BF16), ((3, 2, 2, 32, FC), BF16),
            ((2, 2, 2, 32, 1152), BF16), ((2, 2, 4, 32, 1152), BF16),
            ((2, 2, 16, 1152), BF16), ((2, 2, 32, 1152), BF16),
            ((8, 128), F32), ((3, 8, 128), F32),
        )
    ] + [
        pltpu.SemaphoreType.DMA((12,)),
        pltpu.SemaphoreType.DMA((N_SENDS,)),
        pltpu.SemaphoreType.DMA((N_SENDS,)),
    ]
    outs = pl.pallas_call(
        layer_kernel,
        out_shape=(
            shape((4, R, D), BF16), shape((4, R, D), BF16),
            shape((64, QC), F32), shape((64, 128), F32), shape((64, QC), F32),
            shape((64, FC), F32), shape((64, FC), F32), shape((64, FC), F32),
            shape((1, 64), F32), shape((1, 64), F32),
        ),
        in_specs=[smem] + [any_spec] * 8 + [vmem] * 4,
        out_specs=(vmem,) * 10,
        scratch_shapes=scratch,
        compiler_params=pltpu.CompilerParams(
            collective_id=0, has_side_effects=True, vmem_limit_bytes=65200 * 1024
        ),
    )(
        block_order, hidden_in.reshape(4, R, D), cotangent.reshape(4, R, D),
        w_query, w_keyval, w_output, w_gate.reshape(wide), w_up.reshape(wide), w_down,
        gain_attn.reshape(1, D), gain_ffn.reshape(1, D), coarse, fine,
    )
    bo, gi, g_q, g_kv, g_o, g_g, g_u, g_d, gain_a, gain_f = outs
    return (
        bo.reshape(1, T, D),
        gi.reshape(1, T, D).astype(F32),
        g_q,
        g_kv,
        g_o.T,
        g_g,
        g_u,
        g_d.T,
        gain_a.reshape(64),
        gain_f.reshape(64),
    )


def solution(mesh):
    return jax.shard_map(
        per_device,
        mesh=mesh,
        in_specs=(
            P("dp", "ctx", None),
            P("dp", None),
            P(None, "tensor"),
            P(None, "tensor"),
            P("tensor", None),
            P(None, "tensor"),
            P(None, "tensor"),
            P("tensor", None),
            P(),
            P(),
            P("dp", "ctx", None),
        ),
        out_specs=(
            P("dp", "ctx", None),
            P("dp", "ctx", None),
            P(("dp", "ctx"), "tensor"),
            P(("dp", "ctx"), "tensor"),
            P("tensor", ("dp", "ctx")),
            P(("dp", "ctx"), "tensor"),
            P(("dp", "ctx"), "tensor"),
            P("tensor", ("dp", "ctx")),
            P(("dp", "ctx")),
            P(("dp", "ctx")),
        ),
        check_vma=False,
    )
```

time: 825 us -> 150 us (0.18)
  waiting for transfers between devices: 561 us -> 0 us
  Pallas kernels: 0 us -> 141 us
  blocking collectives: 81.4 us -> 0 us
  matrix products: 77.5 us -> 0 us
  other arithmetic: 51.3 us -> 2.57 us
  local copies, waits for them, and re-layouts: 33.1 us -> 6.07 us
  between operations: 15.1 us -> 0.72 us
    reduce_scatter x6 -> x0, waiting for transfers between devices: 395 us -> none  [the longest x1 87.2 us: per_device(): lax.psum_scatter(grad_up.astype(jnp.bfloat16), ('dp', 'ctx'), scatter_dim...]
    pallas_call x0 -> x1, Pallas kernels: none -> 141 us  [per_device(): pl.pallas_call(layer_kernel, out_shape=(shape((4, R, D), BF16), shape((4,...]
    psum x3 -> x0, waiting for transfers between devices: 132 us -> none  [the longest x1 51.9 us: per_device(): lax.psum(jnp.dot(inner_act, w_down, preferred_element_type=jnp.float32).a...]
    dot_general x60 -> x0, matrix products: 77.5 us -> none  [the longest x9 13.4 us: masked_scores(): jnp.einsum('qgd,kd->gqk', queries, key_piece[:, :head_size], preferred_el...]
    unnamed x1 -> x0, blocking collectives: 68 us -> none
    ppermute x15 -> x0, waiting for transfers between devices: 34.2 us -> none  [shifted(): return lax.ppermute(x, axis, [(i, (i + by) % peers) for i in range(peers)])]
    reduce_sum x15 -> x0, other arithmetic: 17.6 us -> none  [the longest x9 5.95 us: positions(): jnp.sum(jnp.where(slot_index[:, None] == slot_table[None, :], order_row[N...]
    while x35 -> x0, local copies, waits for them, and re-layouts: 14 us -> none
  transfers between devices with their start and end apart: 24 -> 0, of which waited for: 17 -> 0; matrix products, arithmetic and copies ran while one was open for 10% -> 0% of each run, Pallas kernels for 0% -> 0%
where the time goes in v1:
time: 150 us
  Pallas kernels  141 us (94%)
  local copies, waits for them, and re-layouts  6.07 us (4%)
  other arithmetic  2.57 us (2%)
    pallas_call x1, Pallas kernels, per_device(): pl.pallas_call(layer_kernel, out_shape=(shape((4, R, D), BF16), shape((4,...  141 us
    unnamed x27, local copies, waits for them, and re-layouts  6.07 us

profile of v1, /device:TPU:0, one launch (start us, length us, event | category | flops | bytes accessed | tf_op | source)
XLA Modules:
  0.0 150.0 jit_solution(15006118459880830852)
XLA Ops:
  0.6 140.6 %shard_map.204 = (bf16[4,48,2048]{2,1,0:T(8,128)(2,1)}, bf16[4,48,2048]{2,1,0:T(8,128)(2,1)}, f32[64,512]{1,0:T(8,128)}, f32[64,128]{1,0:T(8,128)}, f32[64,512]{...) custom-call(s32[1,16]{1,0:T(1,128)} %order.1, ...), custom_call_target="tpu_custom_call" | custom-call | tf_op jit(solution)/shard_map/pallas_call | solution.py:645
  141.3 0.0 copy-start
  141.3 0.0 copy-start.5
  141.3 0.0 copy-start.6
  141.3 0.0 copy-start.4
  141.3 0.0 copy-start.3
  141.3 0.0 copy-start.2
  141.3 2.6 %bitcast_convert_fusion = f32[1,192,2048]{2,1,0:T(8,128)} fusion(bf16[1,192,2048]{2,1,0:T(8,128)(2,1)} %bitcast.20), kind=kLoop, calls=%fused_computation | loop fusion | flops 393216 | bytes 2359296 | tf_op jit(solution)/shard_map/convert_element_type | solution.py:667
  143.9 0.0 copy-done
  143.9 0.0 copy-start.1
  143.9 0.0 copy-start.8
  143.9 0.0 copy-start.7
  143.9 0.9 copy.32
  144.8 0.0 copy-done.5
  144.8 0.7 copy.33
  145.5 0.0 copy-done.6
  145.5 0.6 copy.34
  146.1 0.0 copy-done.4
  146.1 0.7 copy.35
  146.7 0.0 copy-done.3
  146.7 0.7 copy.36
  147.5 0.0 copy-done.2
  147.5 0.7 copy.37
  148.2 0.0 copy-done.1
  148.2 0.7 copy.38
  149.0 0.0 copy-done.8
  149.0 0.5 copy.39
  149.5 0.0 copy-done.7
  149.5 0.5 copy.40
Async XLA Ops:
  141.3 2.6 %copy-start = (bf16[4,48,2048]{2,1,0:T(8,128)(2,1)S(1)}, bf16[4,48,2048]{2,1,0:T(8,128)(2,1)}, u32[]{:S(2)}) copy-start(bf16[4,48,2048]{2,1,0:T(8,128)(2,1)} %get-tuple-element.20) | copy-start | bytes 2359300
  141.3 3.5 %copy-start.5 = (f32[64,512]{1,0:T(8,128)S(1)}, f32[64,512]{1,0:T(8,128)}, u32[]{:S(2)}) copy-start(f32[64,512]{1,0:T(8,128)} %get-tuple-element.42) | copy-start | bytes 393220
  141.3 4.2 %copy-start.6 = (f32[64,128]{1,0:T(8,128)S(1)}, f32[64,128]{1,0:T(8,128)}, u32[]{:S(2)}) copy-start(f32[64,128]{1,0:T(8,128)} %get-tuple-element.43) | copy-start | bytes 98308
  141.3 4.8 %copy-start.4 = (f32[64,512]{1,0:T(8,128)S(1)}, f32[64,512]{1,0:T(8,128)}, u32[]{:S(2)}) copy-start(f32[64,512]{1,0:T(8,128)} %get-tuple-element.24) | copy-start | bytes 393220
  141.3 5.4 %copy-start.3 = (f32[64,1408]{1,0:T(8,128)S(1)}, f32[64,1408]{1,0:T(8,128)}, u32[]{:S(2)}) copy-start(f32[64,1408]{1,0:T(8,128)} %get-tuple-element.45) | copy-start | bytes 1081348
  141.3 6.2 %copy-start.2 = (f32[64,1408]{1,0:T(8,128)S(1)}, f32[64,1408]{1,0:T(8,128)}, u32[]{:S(2)}) copy-start(f32[64,1408]{1,0:T(8,128)} %get-tuple-element.46) | copy-start | bytes 1081348
  143.9 4.3 %copy-start.1 = (f32[64,1408]{1,0:T(8,128)S(1)}, f32[64,1408]{1,0:T(8,128)}, u32[]{:S(2)}) copy-start(f32[64,1408]{1,0:T(8,128)} %get-tuple-element.27) | copy-start | bytes 1081348
  143.9 5.0 %copy-start.8 = (f32[1,64]{1,0:T(1,128)S(1)}, f32[1,64]{1,0:T(1,128)}, u32[]{:S(2)}) copy-start(f32[1,64]{1,0:T(1,128)} %get-tuple-element.28) | copy-start | bytes 772
  143.9 5.6 %copy-start.7 = (f32[1,64]{1,0:T(1,128)S(1)}, f32[1,64]{1,0:T(1,128)}, u32[]{:S(2)}) copy-start(f32[1,64]{1,0:T(1,128)} %get-tuple-element.29) | copy-start | bytes 772

commit v2 on v1

v2 whole, which is shorter than its diff:
```python
import jax
import jax.numpy as jnp
import numpy as np
from jax import lax
from jax.experimental import pallas as pl
from jax.experimental.pallas import tpu as pltpu
from jax.sharding import PartitionSpec as P

MESH = pl.DeviceIdType.MESH
F32 = jnp.float32
BF16 = jnp.bfloat16
EPSILON = 1e-05
NEG_FILL = -1e30
ROPE_BASE = 10000.0

D = 2048
HD = 64
T = 192
BLOCK = 96
TA = 128
R = 48
QC = 512
FC = 1408
KEYS = 1536
PAIRS = 4
QUERIES = 1536
CHUNK = 512
GROUP = 768
CHIP_KEYS = 384
FF_TILES = ((0, 384), (384, 384), (768, 384), (1152, 256))


def rope_tables():
    half = HD // 2
    freq = ROPE_BASE ** (-np.arange(half, dtype=np.float64) / half)
    freq = np.tile(freq, 4)[None, :]
    coarse = np.arange(16, dtype=np.float64)[:, None] * BLOCK * freq
    fine = np.arange(BLOCK, dtype=np.float64)[:, None] * freq
    coarse = np.stack([np.cos(coarse), np.sin(coarse)]).astype(np.float32)
    fine = np.stack([np.cos(fine), np.sin(fine)]).astype(np.float32)
    return coarse, fine


def dot(a, b):
    return jnp.dot(a, b, preferred_element_type=F32)


def dot_nt(a, b):
    return lax.dot_general(a, b, (((1,), (1,)), ((), ())), preferred_element_type=F32)


def tiles(total, size):
    return [(s, min(size, total - s)) for s in range(0, total, size)]


def lane_of(shape):
    return lax.broadcasted_iota(jnp.int32, shape, len(shape) - 1)


def swap_halves(t):
    first = lane_of(t.shape) % HD < HD // 2
    return jnp.where(first, pltpu.roll(t, 96, 1), pltpu.roll(t, 32, 1))


def layer_kernel(
    order, x_h, c_h, wq_h, wkv_h, wo_h, wg_h, wu_h, wd_h, ga, gf, coarse, fine,
    bo, gi, o_q, o_kv, o_o, o_g, o_u, o_d, gain_a, gain_f,
    x, cot, wq, wkv, wo, wg, wu, wd, row_g, row_u, row_q, row_kv,
    xn, kvall, kk, vv, kt, vt, qst, cos_t, sin_t, s_buf, pt, ob, rl,
    zs, zr, mid, dmid, hn, da, bo_s, gi_s, dinner, act, act_p, g_first,
    xn_t, c_t, hn_t, xn_p, c_p, hn_p, da_p, ob_p, dqp, dqp_p, dkvp, dkvp_p,
    dkv_r, delta, r1f, r2f, r3f, r4f, r1a, r2a, r3a, r4a,
    g_q, g_kv, g_o, g_g, g_u, g_d, gain_s, gain_r,
    local_sem, send_sem, recv_sem,
):
    iy = lax.axis_index("dp")
    ictx = lax.axis_index("ctx")
    iz = lax.axis_index("tensor")
    ix = ictx // 2
    core = ictx % 2
    other = 1 - core

    def z_peer(k):
        return (iy, ictx, (iz + k) % 4)

    def ctx_peer(k):
        return (iy, (ictx + k) % 8, iz)

    def x_peer(k):
        return (iy, ((ix + k) % 4) * 2 + core, iz)

    def y_peer(k):
        return ((iy + k) % 4, ictx, iz)

    core_peer = (iy, ix * 2 + other, iz)

    local = []
    local_done = set()

    def copy_local(src, dst):
        copy = pltpu.make_async_copy(src, dst, local_sem.at[len(local)])
        copy.start()
        local.append(copy)
        return copy

    def wait_local(*copies):
        for copy in copies:
            copy.wait()
            local_done.add(id(copy))

    x_load = copy_local(x_h, x)
    wkv_load = copy_local(wkv_h, wkv)
    wq_load = copy_local(wq_h, wq)

    barrier = pltpu.get_barrier_semaphore()
    greeted = (
        [ctx_peer(k) for k in range(1, 8)]
        + [z_peer(k) for k in range(1, 4)]
        + [y_peer(1), y_peer(3)]
    )
    for peer in greeted:
        pl.semaphore_signal(barrier, inc=1, device_id=peer, device_id_type=MESH)

    sent = []
    arrived, released = set(), set()

    def send(src, dst, peer):
        n = len(sent)
        copy = pltpu.make_async_remote_copy(
            src_ref=src, dst_ref=dst, send_sem=send_sem.at[n], recv_sem=recv_sem.at[n],
            device_id=peer, device_id_type=MESH,
        )
        copy.start()
        sent.append(copy)
        return copy

    def wait_recv(copies):
        for copy in copies:
            copy.wait_recv()
            arrived.add(id(copy))

    def wait_send(copies):
        for copy in copies:
            copy.wait_send()
            released.add(id(copy))

    pick = lax.broadcasted_iota(jnp.int32, (16, 128), 0)
    sign = jnp.where(lane_of((BLOCK, 128)) % HD < HD // 2, -1.0, 1.0).astype(F32)
    for b in range(2):
        chosen = pick == order[0, ictx * 2 + b]
        ca = jnp.sum(jnp.where(chosen, coarse[0], 0.0), 0, keepdims=True)
        sa = jnp.sum(jnp.where(chosen, coarse[1], 0.0), 0, keepdims=True)
        cos_t[b * BLOCK : (b + 1) * BLOCK, :] = ca * fine[0] - sa * fine[1]
        sin_t[b * BLOCK : (b + 1) * BLOCK, :] = (sa * fine[0] + ca * fine[1]) * sign

    def rot(t):
        return t * cos_t[...] + swap_halves(t) * sin_t[...]

    def rot_back(t):
        return t * cos_t[...] - swap_halves(t) * sin_t[...]

    def inv_rms(v):
        return lax.rsqrt(jnp.mean(v * v, -1, keepdims=True) + EPSILON)

    low_lane = lane_of((T, 128)) < HD
    low_a, low_b = low_lane[0:TA], low_lane[0 : T - TA]

    wait_local(x_load)
    for i in range(4):
        rows = x[i * R : (i + 1) * R, :].astype(F32)
        xn[i * R : (i + 1) * R, :] = (rows * inv_rms(rows) * ga[...]).astype(BF16)
    wait_local(wkv_load)
    cot_load = copy_local(c_h, cot)
    wd_load = copy_local(wd_h, wd)
    normed = xn[...]
    kvp = dot(normed, wkv[...])
    kvall[ictx] = jnp.where(low_lane, rot(kvp), kvp).astype(BF16)
    pl.semaphore_wait(barrier, len(greeted))
    kv_copies = [send(kvall.at[ictx], kvall.at[ictx], ctx_peer(k)) for k in range(1, 8)]
    wait_local(wq_load)
    wo_load = copy_local(wo_h, wo)
    wg_load = copy_local(wg_h, wg)
    wu_load = copy_local(wu_h, wu)
    own_h, own_a, own_b = iy // 2, (iy % 2) * 2 + ix // 2, (ix % 2) * 2 + core
    own_rows = pl.ds(pl.multiple_of(((iy * 4 + ix) * 2 + core) * 64, 64), 64)
    row_loads = [
        copy_local(wg_h.at[own_h, own_a, own_b], row_g),
        copy_local(wu_h.at[own_h, own_a, own_b], row_u),
        copy_local(wq_h.at[own_rows], row_q),
        copy_local(wkv_h.at[own_rows], row_kv),
    ]

    def by_query(pair, value, ref):
        for i in range(2):
            h = pair * 2 + i
            one = jnp.where(low_lane, value, 0.0) if i == 0 else jnp.where(low_lane, 0.0, value)
            one = one.astype(BF16)
            ref[h * TA : (h + 1) * TA, :] = one[0:TA]
            ref[8 * TA + h * 64 : 8 * TA + (h + 1) * 64, :] = one[TA:T]

    for s, n in tiles(QC, 256):
        qp = dot(normed, wq[:, s : s + n])
        for j in range(n // 128):
            by_query(s // 128 + j, rot(qp[:, j * 128 : (j + 1) * 128]) * (HD ** -0.5), qst)

    turned = (4, 4, 2, 2, 32, T)
    xn_t[...] = normed.T.reshape(turned)
    xnt_copy = send(xn_t.at[:, :, other], xn_p, core_peer)
    wait_local(cot_load)
    cot_rows = cot[...]
    c_t[...] = cot_rows.T.reshape(turned)
    ct_copy = send(c_t.at[:, :, other], c_p, core_peer)
    wait_local(wd_load)
    for s, n in tiles(FC, 512):
        dinner[:, s : s + n] = dot_nt(cot_rows, wd[s : s + n, :])

    wait_recv(kv_copies)
    for j in range(8):
        wide = kvall[j].astype(F32)
        rolled = pltpu.roll(wide, HD, 1)
        rows = pl.ds(j * T, T)
        kk[rows, :] = jnp.where(low_lane, wide, rolled).astype(BF16)
        vv[rows, :] = jnp.where(low_lane, rolled, wide).astype(BF16)
    kv_t = kvall[...].reshape(KEYS, 128).T
    kt[0:HD, :] = kv_t[0:HD]
    kt[HD : 2 * HD, :] = kv_t[0:HD]
    vt[0:HD, :] = kv_t[HD : 2 * HD]
    vt[HD : 2 * HD, :] = kv_t[HD : 2 * HD]
    vt[2 * HD : 2 * HD + 16, :] = jnp.ones((16, KEYS), BF16)

    lane = lane_of((1, CHUNK))
    token = lane % TA
    start_0, start_1 = order[0, ictx * 2] * BLOCK, order[0, ictx * 2 + 1] * BLOCK
    place_a = jnp.where(token >= BLOCK, start_1 + token - BLOCK, start_0 + token)
    place_b = start_1 + (TA - BLOCK) + lane % 64
    key_row = lax.broadcasted_iota(jnp.int32, (BLOCK, CHUNK), 0)

    def attend(chunk):
        q_place = place_a if chunk < 2 else place_b
        lanes = slice(chunk * CHUNK, (chunk + 1) * CHUNK)
        top = jnp.full((8, CHUNK), NEG_FILL, F32)
        for r0 in range(0, KEYS, GROUP):
            scores = dot_nt(kk[r0 : r0 + GROUP, :], qst[lanes, :])
            for b in range(GROUP // BLOCK):
                limit = q_place - order[0, r0 // BLOCK + b] * BLOCK
                rows = slice(b * BLOCK, (b + 1) * BLOCK)
                seen = jnp.where(key_row <= limit, scores[rows], NEG_FILL)
                s_buf[r0 + b * BLOCK : r0 + (b + 1) * BLOCK, :] = seen
                top = jnp.maximum(top, jnp.max(seen.reshape(BLOCK // 8, 8, CHUNK), 0))
        top = jnp.max(top, 0, keepdims=True)
        for r0 in range(0, KEYS, GROUP):
            rows = slice(r0, r0 + GROUP)
            pt[rows, lanes] = jnp.exp(s_buf[rows, :] - top).astype(BF16)
        summed = dot(vt[...], pt[:, lanes])
        inv = 1.0 / summed[2 * HD : 2 * HD + 1]
        out = summed[0 : 2 * HD] * inv
        inv = jnp.broadcast_to(inv, (2 * HD, CHUNK))
        if chunk < 2:
            for j in range(2):
                pair = slice((chunk * 2 + j) * 128, (chunk * 2 + j + 1) * 128)
                one, two = slice(j * 256, j * 256 + 128), slice(j * 256 + 128, j * 256 + 256)
                ob[0:TA, pair] = jnp.where(low_a, out[:, one].T, out[:, two].T).astype(BF16)
                rl[0:TA, pair] = jnp.where(low_a, inv[:, one].T, inv[:, two].T)
        else:
            for p in range(PAIRS):
                pair = slice(p * 128, (p + 1) * 128)
                o2, i2 = out[:, pair].T, inv[:, pair].T
                ob[TA:T, pair] = jnp.where(low_b, o2[0:64], o2[64:128]).astype(BF16)
                rl[TA:T, pair] = jnp.where(low_b, i2[0:64], i2[64:128])

    def z_rows(part, z):
        if part == 0:
            return pl.ds(pl.multiple_of(z * 32, 32), 32)
        return pl.ds(pl.multiple_of(TA + z * 16, 16), 16)

    kept = (slice(0, 32), slice(32, 48))
    all_cols = pl.ds(0, D)

    def z_scatter(src, n, part, cols=all_cols):
        return [
            send(
                src.at[z_rows(part, (iz + k) % 4), cols], zr.at[n, k - 1, kept[part], cols],
                z_peer(k),
            )
            for k in (2, 1, 3)
        ]

    def z_sum(src, n, part):
        total = src[z_rows(part, iz), :].astype(F32)
        for k in range(3):
            total = total + zr[n, k, kept[part], :].astype(F32)
        return total

    def z_gather(buf, part, own=None):
        rows = z_rows(part, iz)
        src = buf.at[rows] if own is None else own.at[kept[part]]
        return [send(src, buf.at[rows], z_peer(k)) for k in (2, 1, 3)]

    def project_out(part):
        rows = slice(0, TA) if part == 0 else slice(TA, T)
        copies = []
        for s, n in tiles(D, 1024):
            zs[rows, s : s + n] = dot(ob[rows, :], wo[:, s : s + n]).astype(BF16)
            copies += z_scatter(zs, 0, part, pl.ds(s, n))
        return copies

    attend(0)
    attend(1)
    wait_local(wo_load)
    attn_copies = [project_out(0)]
    attend(2)
    attn_copies.append(project_out(1))
    ob_copy = send(ob, ob_p, core_peer)

    hn_copies = []
    for part in range(2):
        wait_recv(attn_copies[part])
        m = x[z_rows(part, iz), :].astype(F32) + z_sum(zs, 0, part)
        mid[kept[part], :] = m
        hn[z_rows(part, iz), :] = (m * inv_rms(m) * gf[...]).astype(BF16)
        hn_copies += z_gather(hn, part)

    wait_local(wg_load, wu_load)
    wait_recv(hn_copies)
    hidden = hn[...]
    act_copies = [[], [], []]
    for s, n in FF_TILES:
        cols = slice(s, s + n)
        g = dot(hidden, wg[:, :, :, :, :, cols].reshape(D, n))
        u = dot(hidden, wu[:, :, :, :, :, cols].reshape(D, n))
        sig = 1.0 / (1.0 + jnp.exp(-g))
        a = g * sig
        di = dinner[:, cols]
        act[0, :, cols] = (a * u).astype(BF16)
        act[1, :, cols] = (di * u * sig * (1.0 + g * (1.0 - sig))).astype(BF16)
        act[2, :, cols] = (di * a).astype(BF16)
        for i in range(3):
            act_copies[i].append(
                send(act.at[i, :, pl.ds(s, n)], act_p.at[i, :, pl.ds(s, n)], core_peer)
            )

    xp, xm, x2 = (ix + 1) % 4, (ix + 3) % 4, (ix + 2) % 4
    yp, ym, y2 = (iy + 1) % 4, (iy + 3) % 4, (iy + 2) % 4

    def own_part(ref):
        return lambda dy, dx, h: ref[dy, dx, core, h]

    def partner_part(ref):
        return lambda dy, dx, h: ref[dy, dx, h]

    all4 = pl.ds(0, 4)
    first_rows = [(all4, x2, 0), (y2, all4, 1)]
    other_rows = [(all4, dx, 0) for dx in (xp, xm, ix)] + [(dy, all4, 1) for dy in (yp, ym, iy)]

    def weight_grad(part, which, own_t, partner_t, own_b, partner_b, store=None, c0=0, n=None):
        ref, half, part_c0, part_n, _, _ = parts[part]
        n = part_n if n is None else n
        get_own, get_partner = own_part(own_t), partner_part(partner_t)
        a_own = jnp.concatenate([get_own(*i).reshape(128, T) for i in which], 0)
        a_partner = jnp.concatenate([get_partner(*i).reshape(128, T) for i in which], 0)
        for s, w in tiles(n, 256):
            r = dot(a_own, own_b[:, s : s + w]) + dot(a_partner, partner_b[:, s : s + w])
            r = r.astype(BF16)
            cols = slice(part_c0 + c0 + s, part_c0 + c0 + s + w)
            for i, (dy, dx, h) in enumerate(which):
                rows = r[i * 128 : (i + 1) * 128].reshape(4, 32, w)
                if store is None:
                    ref[half, dy, dx, h, :, cols] = rows
                else:
                    store[i, :, :, cols] = rows

    f_bufs = [[r.at[i] for r in (r1f, r2f, r3f, r4f)] for i in range(3)]
    a_bufs = [r1a, r2a, r3a, r4a]
    parts = [
        (wg, 1, 0, FC, f_bufs[0], 0),
        (wg, 0, 0, FC, f_bufs[1], 0),
        (wu, 0, 0, FC, f_bufs[2], 0),
        (wu, 1, 0, 512, a_bufs, 0),
        (wu, 1, 512, 640, a_bufs, 512),
    ]
    flights = {}
    lo2, hi2 = pl.ds(0, 2), pl.ds(2, 2)
    all32, lo16, hi16 = pl.ds(0, 32), pl.ds(0, 16), pl.ds(16, 16)

    def g_index(part, dy, dx, h, rows=None):
        ref, half, c0, n, _, _ = parts[part]
        return (half, dy, dx, h, all32 if rows is None else rows, pl.ds(c0, n))

    def outgoing(part, step):
        if step == 0 and part == 0:
            return (
                (g_first.at[0, lo2], g_first.at[0, hi2]),
                (g_first.at[1, lo2], g_first.at[1, hi2]),
            )
        if step == 0:
            index = (
                (g_index(part, lo2, x2, 0), g_index(part, hi2, x2, 0)),
                (g_index(part, y2, lo2, 1), g_index(part, y2, hi2, 1)),
            )
        elif step == 1:
            index = (
                (g_index(part, all4, xp, 0), g_index(part, all4, xm, 0)),
                (g_index(part, yp, all4, 1), g_index(part, ym, all4, 1)),
            )
        elif step == 2:
            index = (
                (g_index(part, y2, ix, 0, lo16), g_index(part, y2, ix, 0, hi16)),
                (g_index(part, iy, x2, 1, lo16), g_index(part, iy, x2, 1, hi16)),
            )
        else:
            index = (
                (g_index(part, yp, ix, 0), g_index(part, ym, ix, 0)),
                (g_index(part, iy, xp, 1), g_index(part, iy, xm, 1)),
            )
        ref = parts[part][0]
        return tuple(tuple(ref.at[i] for i in flow) for flow in index)

    def landing(part, step, flow, way):
        _, _, _, n, bufs, b0 = parts[part]
        return bufs[step].at[flow, way, ..., pl.ds(b0, n)]

    def rs_send(part, step):
        out = outgoing(part, step)
        for flow in range(2):
            along_x = (flow == 0) == (step < 2)
            for way, k in ((0, 1), (1, 3)):
                peer = x_peer(k) if along_x else y_peer(k)
                flights[part, step, flow, way] = send(
                    out[flow][way], landing(part, step, flow, way), peer
                )

    def add_in(ref, index, *arrived):
        total = ref[index].astype(F32)
        for a in arrived:
            total = total + a[...].astype(F32)
        ref[index] = total.astype(BF16)

    def rs_recv(part, step):
        ref = parts[part][0]
        for flow in range(2):
            wait_recv([flights[part, step, flow, way] for way in range(2)])
            got = [landing(part, step, flow, way) for way in range(2)]
            if step == 0:
                if flow == 0:
                    add_in(ref, g_index(part, lo2, xp, 0), got[0])
                    add_in(ref, g_index(part, hi2, xm, 0), got[1])
                else:
                    add_in(ref, g_index(part, yp, lo2, 1), got[0])
                    add_in(ref, g_index(part, ym, hi2, 1), got[1])
            elif step == 1:
                if flow == 0:
                    add_in(ref, g_index(part, all4, ix, 0), *got)
                else:
                    add_in(ref, g_index(part, iy, all4, 1), *got)
            elif step == 2:
                if flow == 0:
                    add_in(ref, g_index(part, yp, ix, 0, lo16), got[0])
                    add_in(ref, g_index(part, ym, ix, 0, hi16), got[1])
                else:
                    add_in(ref, g_index(part, iy, xp, 1, lo16), got[0])
                    add_in(ref, g_index(part, iy, xm, 1, hi16), got[1])

    def rs_turn(part, step):
        rs_recv(part, step)
        rs_send(part, step + 1)

    def rs_last(part, outs):
        rs_recv(part, 3)
        ref = parts[part][0]
        for flow in range(2):
            total = ref[g_index(part, iy, ix, flow)].astype(F32)
            for way in range(2):
                total = total + landing(part, 3, flow, way)[...].astype(F32)
            for stage, out, s, n in outs:
                stage[flow * 32 : (flow + 1) * 32, :] = total[:, s : s + n]
        for stage, out, s, n in outs:
            copy_local(stage, out)

    hn_t[...] = hidden.T.reshape(turned)
    hnt_copy = send(hn_t.at[:, :, other], hn_p, core_peer)
    wait_recv([ct_copy] + act_copies[0])
    weight_grad(0, first_rows, c_t, c_p, act.at[0], act_p.at[0], store=g_first)
    rs_send(0, 0)

    wait_send([copy for copies in attn_copies for copy in copies])
    dhn_copies = [[], []]
    for t in range(4):
        cols = slice(t * 512, (t + 1) * 512)
        block = (t // 2, slice((t % 2) * 2, (t % 2) * 2 + 2))
        r = dot_nt(act[1], wg[block].reshape(512, FC)) + dot_nt(act[2], wu[block].reshape(512, FC))
        zs[:, cols] = r.astype(BF16)
        dhn_copies[0] += z_scatter(zs, 1, 0, pl.ds(t * 512, 512))
    dhn_copies[1] += z_scatter(zs, 1, 1)
    wait_recv([hnt_copy] + act_copies[1])
    weight_grad(1, first_rows, hn_t, hn_p, act.at[1], act_p.at[1])
    rs_send(1, 0)
    wait_recv(act_copies[2])
    weight_grad(2, first_rows, hn_t, hn_p, act.at[2], act_p.at[2])
    rs_send(2, 0)
    weight_grad(0, other_rows, c_t, c_p, act.at[0], act_p.at[0])
    rs_turn(0, 0)

    da_copies = []

    def norm_back(part):
        wait_recv(dhn_copies[part])
        m = mid[kept[part], :]
        r2 = inv_rms(m)
        mhat = m * r2
        scaled = z_sum(zs, 1, part) * gf[...]
        rows = z_rows(part, iz)
        dm = cot[rows, :].astype(F32) + r2 * (
            scaled - mhat * jnp.mean(scaled * mhat, -1, keepdims=True)
        )
        dmid[kept[part], :] = dm
        da[rows, :] = dm.astype(BF16)
        da_copies.extend(z_gather(da, part))

    norm_back(0)
    weight_grad(1, other_rows, hn_t, hn_p, act.at[1], act_p.at[1])
    norm_back(1)
    weight_grad(2, other_rows, hn_t, hn_p, act.at[2], act_p.at[2])
    rs_turn(1, 0)
    inner = act[0]
    for s, n in tiles(D, 512):
        xn[:, s : s + n] = dot(inner, wd[:, s : s + n]).astype(BF16)
    rs_turn(2, 0)

    wait_recv(da_copies)
    ffn_copies = [z_scatter(xn, 2, part) for part in range(2)]
    grad_attn = da[...]
    for s, n in tiles(QC, 256):
        grad_rows = dot_nt(grad_attn, wo[s : s + n, :])
        for j in range(n // 128):
            p = s // 128 + j
            pair = slice(p * 128, (p + 1) * 128)
            g = grad_rows[:, j * 128 : (j + 1) * 128] * rl[:, pair]
            by_query(p, g, kk)
            by_row = (g * ob[:, pair].astype(F32)).T
            for i in range(2):
                h = p * 2 + i
                sums = jnp.sum(by_row[i * HD : (i + 1) * HD], 0, keepdims=True)
                delta[:, h * TA : (h + 1) * TA] = sums[:, 0:TA]
                delta[:, 8 * TA + h * 64 : 8 * TA + (h + 1) * 64] = sums[:, TA:T]
    wait_send([ct_copy])
    c_t[...] = grad_attn.T.reshape(turned)
    dat_copy = send(c_t.at[:, :, other], da_p, core_peer)
    dob = kk

    wait_send(kv_copies)
    dkv_copies = []
    for i, step in enumerate((2, 1, 3, 0)):
        chip = (ix + step) % 4
        rows = pl.ds(pl.multiple_of(chip * CHIP_KEYS, CHIP_KEYS), CHIP_KEYS)
        weights = pt[rows, :]
        dv = dot(weights, dob[...])
        for s, n in tiles(QUERIES, CHUNK):
            lanes = slice(s, s + n)
            grad_weights = dot_nt(vv[rows, :], dob[lanes, :])
            pt[rows, lanes] = (
                weights[:, lanes].astype(F32) * (grad_weights - delta[:, lanes])
            ).astype(BF16)
        dk = dot(pt[rows, :], qst[...])
        both = jnp.where(
            lane_of((CHIP_KEYS, 128)) < HD, dk + pltpu.roll(dk, HD, 1), dv + pltpu.roll(dv, HD, 1)
        ).astype(BF16)
        for c in range(2):
            kvall[chip * 2 + c] = both[c * T : (c + 1) * T]
        for c, goal in ((0, core), (1, other)):
            if step != 0 or c == 1:
                dkv_copies.append(
                    send(kvall.at[chip * 2 + goal], dkv_r.at[i, c], (iy, chip * 2 + goal, iz))
                )
        if i == 1:
            wait_recv([dat_copy, ob_copy])
            weight_grad(3, first_rows, c_t, da_p, ob, ob_p)
            rs_send(3, 0)
    dq_t = dot(kt[...], pt[...]) * (HD ** -0.5)
    for p in range(PAIRS):
        a0 = dq_t[:, p * 256 : p * 256 + 128].T
        a1 = dq_t[:, p * 256 + 128 : p * 256 + 256].T
        b = dq_t[:, 8 * TA + p * 128 : 8 * TA + (p + 1) * 128].T
        dq = jnp.concatenate(
            [jnp.where(low_a, a0, a1), jnp.where(low_b, b[0:64], b[64:128])], 0
        )
        dqp[:, p * 128 : (p + 1) * 128] = rot_back(dq).astype(BF16)
    dqp_copy = send(dqp, dqp_p, core_peer)

    wait_recv(dkv_copies)
    home = kvall[ictx].astype(F32) + dkv_r[3, 1].astype(F32)
    for i in range(3):
        for c in range(2):
            home = home + dkv_r[i, c].astype(F32)
    dkvp[...] = jnp.where(low_lane, rot_back(home), home).astype(BF16)
    dkvp_copy = send(dkvp, dkvp_p, core_peer)
    wait_send([copy for copies in dhn_copies for copy in copies])
    q_rows, kv_rows = dqp[...], dkvp[...]
    dxn_copies = [[], []]
    for s, n in tiles(D, 512):
        r = dot_nt(q_rows, wq[s : s + n, :]) + dot_nt(kv_rows, wkv[s : s + n, :])
        zs[:, s : s + n] = r.astype(BF16)
        dxn_copies[0] += z_scatter(zs, 3, 0, pl.ds(s, n))
    dxn_copies[1] += z_scatter(zs, 3, 1)

    wait_recv([xnt_copy, dqp_copy])
    weight_grad(4, first_rows, xn_t, xn_p, dqp, dqp_p, c0=0, n=512)
    wait_recv([dkvp_copy])
    weight_grad(4, first_rows, xn_t, xn_p, dkvp, dkvp_p, c0=512, n=128)
    rs_send(4, 0)
    rs_turn(0, 1)
    weight_grad(3, other_rows, c_t, da_p, ob, ob_p)
    weight_grad(4, other_rows, xn_t, xn_p, dqp, dqp_p, c0=0, n=512)
    weight_grad(4, other_rows, xn_t, xn_p, dkvp, dkvp_p, c0=512, n=128)
    rs_turn(1, 1)

    own_rows_out = []
    bo_copies = []
    for part in range(2):
        wait_recv(ffn_copies[part])
        bo_s[kept[part], :] = (mid[kept[part], :] + z_sum(xn, 2, part)).astype(BF16)
        copy_local(bo_s.at[kept[part]], bo.at[z_rows(part, iz)])
        bo_copies += z_gather(bo, part, bo_s)

    rs_turn(3, 0)
    rs_turn(4, 0)

    for part in range(2):
        wait_recv(dxn_copies[part])
        rows = x[z_rows(part, iz), :].astype(F32)
        r1 = inv_rms(rows)
        xhat = rows * r1
        scaled = z_sum(zs, 3, part) * ga[...]
        gi_s[kept[part], :] = (
            dmid[kept[part], :]
            + r1 * (scaled - xhat * jnp.mean(scaled * xhat, -1, keepdims=True))
        ).astype(BF16)
        copy_local(gi_s.at[kept[part]], gi.at[z_rows(part, iz)])
        z_gather(gi, part, gi_s)

    rs_turn(2, 1)
    rs_turn(0, 2)
    rs_turn(1, 2)
    rs_turn(3, 1)
    rs_turn(4, 1)
    rs_turn(2, 2)
    rs_last(0, [(g_d, o_d, 0, FC)])
    rs_last(1, [(g_g, o_g, 0, FC)])
    rs_turn(3, 2)
    rs_turn(4, 2)
    rs_last(2, [(g_u, o_u, 0, FC)])
    rs_last(3, [(g_o, o_o, 0, 512)])
    rs_last(4, [(g_q, o_q, 0, 512), (g_kv, o_kv, 512, 128)])

    wait_local(*row_loads)

    def row_products(pairs):
        total = jnp.zeros((64, 128), F32)
        for grad, weight in pairs:
            n = grad.shape[-1]
            w = weight[...].reshape(64, n)
            for s, _ in tiles(n, 128):
                total = total + grad[:, s : s + 128] * w[:, s : s + 128].astype(F32)
        return jnp.sum(total.T, 0, keepdims=True)

    gain_s[...] = jnp.zeros((8, 128), F32)
    gain_s[0:1, 0:64] = row_products([(g_g, row_g), (g_u, row_u)])
    gain_s[1:2, 0:64] = row_products([(g_q, row_q), (g_kv, row_kv)])
    gain_copies = [send(gain_s, gain_r.at[k - 1], z_peer(k)) for k in range(1, 4)]
    wait_recv(gain_copies)
    total = gain_s[...]
    for k in range(3):
        total = total + gain_r[k]
    chip_cols = pl.ds(pl.multiple_of((iy * 4 + ix) * 128, 128), 128)

    def own_gain(ref):
        v = ref[:, chip_cols]
        return jnp.where(core == 1, pltpu.roll(v, 64, 1), v)[:, 0:64]

    gain_f[...] = total[0:1, 0:64] / own_gain(gf)
    gain_a[...] = total[1:2, 0:64] / own_gain(ga)

    wait_recv([copy for copy in sent if id(copy) not in arrived])
    wait_send([copy for copy in sent if id(copy) not in released])
    wait_local(*[copy for copy in local if id(copy) not in local_done])


def store_kernel(*refs):
    n = 10
    src, dst, held = refs[:n], refs[n : 2 * n], refs[2 * n : 3 * n]
    wide, in_sem, out_sem = refs[3 * n :]
    moves = []
    for i in range(n):
        if i < 2:
            for j in range(4):
                rows = pl.ds(j * R, R)
                moves.append((src[i].at[rows], held[i].at[rows], dst[i].at[rows], (i, rows)))
        else:
            moves.append((src[i], held[i], dst[i], (i, None)))
    moves.sort(key=lambda move: move[3][0] != 1)
    fetches = []
    for k, (a, b, _, _) in enumerate(moves):
        copy = pltpu.make_async_copy(a, b, in_sem.at[k])
        copy.start()
        fetches.append(copy)
    stores = []
    for k, (_, b, c, (i, rows)) in enumerate(moves):
        fetches[k].wait()
        if i == 1:
            wide[rows, :] = b[...].astype(F32)
            b = wide.at[rows]
        copy = pltpu.make_async_copy(b, c, out_sem.at[k])
        copy.start()
        stores.append(copy)
    for copy in stores:
        copy.wait()


N_SENDS = 224
N_LOCAL = 40


def per_device(
    hidden_in, block_order, w_query, w_keyval, w_output, w_gate, w_up, w_down,
    gain_attn, gain_ffn, cotangent,
):
    coarse, fine = rope_tables()
    any_spec = pl.BlockSpec(memory_space=pl.ANY)
    vmem = pl.BlockSpec(memory_space=pltpu.VMEM)
    smem = pl.BlockSpec(memory_space=pltpu.SMEM)
    shape = jax.ShapeDtypeStruct
    wide = (2, 4, 4, 2, 32, FC)
    turned = (4, 4, 2, 2, 32, T)
    half_turned = (4, 4, 2, 32, T)
    scratch = [
        pltpu.VMEM(s, t)
        for s, t in (
            ((T, D), BF16), ((T, D), BF16),
            ((D, QC), BF16), ((D, 128), BF16), ((QC, D), BF16),
            (wide, BF16), (wide, BF16), ((FC, D), BF16),
            ((2, 32, FC), BF16), ((2, 32, FC), BF16), ((64, QC), BF16), ((64, 128), BF16),
            ((T, D), BF16), ((8, T, 128), BF16),
            ((KEYS, 128), BF16), ((KEYS, 128), BF16),
            ((128, KEYS), BF16), ((144, KEYS), BF16),
            ((QUERIES, 128), BF16), ((T, 128), F32), ((T, 128), F32),
            ((KEYS, CHUNK), F32), ((KEYS, QUERIES), BF16),
            ((T, QC), BF16), ((T, QC), F32),
            ((T, D), BF16), ((4, 3, R, D), BF16),
            ((R, D), F32), ((R, D), F32),
            ((T, D), BF16), ((T, D), BF16), ((R, D), BF16), ((R, D), BF16),
            ((T, FC), F32), ((3, T, FC), BF16), ((3, T, FC), BF16),
            ((2, 4, 32, FC), BF16),
            (turned, BF16), (turned, BF16), (turned, BF16),
            (half_turned, BF16), (half_turned, BF16), (half_turned, BF16), (half_turned, BF16),
            ((T, QC), BF16), ((T, QC), BF16), ((T, QC), BF16),
            ((T, 128), BF16), ((T, 128), BF16),
            ((4, 2, T, 128), BF16), ((1, QUERIES), F32),
            ((3, 2, 2, 2, 32, FC), BF16), ((3, 2, 2, 4, 32, FC), BF16),
            ((3, 2, 2, 16, FC), BF16), ((3, 2, 2, 32, FC), BF16),
            ((2, 2, 2, 32, 1152), BF16), ((2, 2, 4, 32, 1152), BF16),
            ((2, 2, 16, 1152), BF16), ((2, 2, 32, 1152), BF16),
            ((64, QC), F32), ((64, 128), F32), ((64, QC), F32),
            ((64, FC), F32), ((64, FC), F32), ((64, FC), F32),
            ((8, 128), F32), ((3, 8, 128), F32),
        )
    ] + [
        pltpu.SemaphoreType.DMA((N_LOCAL,)),
        pltpu.SemaphoreType.DMA((N_SENDS,)),
        pltpu.SemaphoreType.DMA((N_SENDS,)),
    ]
    grads = (
        shape((64, QC), F32), shape((64, 128), F32), shape((64, QC), F32),
        shape((64, FC), F32), shape((64, FC), F32), shape((64, FC), F32),
        shape((1, 64), F32), shape((1, 64), F32),
    )
    outs = pl.pallas_call(
        layer_kernel,
        out_shape=(shape((T, D), BF16), shape((T, D), BF16)) + grads,
        in_specs=[smem] + [any_spec] * 8 + [vmem] * 4,
        out_specs=(any_spec,) * 8 + (vmem,) * 2,
        scratch_shapes=scratch,
        compiler_params=pltpu.CompilerParams(
            collective_id=0, has_side_effects=True, vmem_limit_bytes=65200 * 1024
        ),
    )(
        block_order, hidden_in.reshape(T, D), cotangent.reshape(T, D),
        w_query, w_keyval, w_output, w_gate.reshape(wide), w_up.reshape(wide), w_down,
        gain_attn.reshape(1, D), gain_ffn.reshape(1, D), coarse, fine,
    )
    outs = pl.pallas_call(
        store_kernel,
        out_shape=(shape((T, D), BF16), shape((T, D), F32)) + grads,
        in_specs=[any_spec] * 10,
        out_specs=(any_spec,) * 10,
        scratch_shapes=[pltpu.VMEM((T, D), BF16)] * 2
        + [pltpu.VMEM(g.shape, F32) for g in grads]
        + [
            pltpu.VMEM((T, D), F32),
            pltpu.SemaphoreType.DMA((16,)), pltpu.SemaphoreType.DMA((16,)),
        ],
        compiler_params=pltpu.CompilerParams(vmem_limit_bytes=65200 * 1024),
    )(*outs)
    bo, gi, g_q, g_kv, g_o, g_g, g_u, g_d, gain_a, gain_f = outs
    return (
        bo.reshape(1, T, D),
        gi.reshape(1, T, D),
        g_q,
        g_kv,
        g_o.T,
        g_g,
        g_u,
        g_d.T,
        gain_a.reshape(64),
        gain_f.reshape(64),
    )


def solution(mesh):
    return jax.shard_map(
        per_device,
        mesh=mesh,
        in_specs=(
            P("dp", "ctx", None),
            P("dp", None),
            P(None, "tensor"),
            P(None, "tensor"),
            P("tensor", None),
            P(None, "tensor"),
            P(None, "tensor"),
            P("tensor", None),
            P(),
            P(),
            P("dp", "ctx", None),
        ),
        out_specs=(
            P("dp", "ctx", None),
            P("dp", "ctx", None),
            P(("dp", "ctx"), "tensor"),
            P(("dp", "ctx"), "tensor"),
            P("tensor", ("dp", "ctx")),
            P(("dp", "ctx"), "tensor"),
            P(("dp", "ctx"), "tensor"),
            P("tensor", ("dp", "ctx")),
            P(("dp", "ctx")),
            P(("dp", "ctx")),
        ),
        check_vma=False,
    )
```

time: 150 us -> 126 us (0.84)
  Pallas kernels: 141 us -> 125 us
  local copies, waits for them, and re-layouts: 6.07 us -> 0 us
  other arithmetic: 2.57 us -> 0 us
    pallas_call x1 -> x2, Pallas kernels: 141 us -> 125 us  [the longest x1 122 us: per_device(): pl.pallas_call(layer_kernel, out_shape=(shape((T, D), BF16), shape((T, D)...]
    unnamed x27 -> x0, local copies, waits for them, and re-layouts: 6.07 us -> none
    convert_element_type x1 -> x0, other arithmetic: 2.57 us -> none  [per_device(): gi.reshape(1, T, D).astype(F32)]
where the time goes in v2:
time: 126 us
  Pallas kernels  125 us (99%)
    pallas_call x1, Pallas kernels, per_device(): pl.pallas_call(layer_kernel, out_shape=(shape((T, D), BF16), shape((T, D)...  122 us
    pallas_call x1, Pallas kernels, per_device(): pl.pallas_call(store_kernel, out_shape=(shape((T, D), BF16), shape((T, D)...  3.09 us

profile of v2, /device:TPU:0, one launch (start us, length us, event | category | flops | bytes accessed | tf_op | source)
XLA Modules:
  0.0 126.1 jit_solution(1402901772891980331)
XLA Ops:
  0.6 122.2 %shard_map.204 = (bf16[192,2048]{1,0:T(8,128)(2,1)}, bf16[192,2048]{1,0:T(8,128)(2,1)}, f32[64,512]{1,0:T(8,128)}, f32[64,128]{1,0:T(8,128)}, f32[64,512]{1,0:T(...) custom-call(s32[1,16]{1,0:T(1,128)} %order.1, ...), custom_call_target="tpu_custom_call" | custom-call | tf_op jit(solution)/shard_map/pallas_call | solution.py:775
  122.9 3.1 %shard_map.205 = (bf16[192,2048]{1,0:T(8,128)(2,1)}, f32[192,2048]{1,0:T(8,128)}, f32[64,512]{1,0:T(8,128)}, f32[64,128]{1,0:T(8,128)}, f32[64,512]{1,0:T(8,128)...) custom-call(bf16[192,2048]{1,0:T(8,128)(2,1)} %get-tuple-element.30.r, ...), custom_call_target="tpu_custom_call" | custom-call | tf_op jit(solution)/shard_map/pallas_call | solution.py:789

commit v3 on v2

--- a/solution.py
+++ b/solution.py
@@ -63,11 +63,11 @@
 
 
 def layer_kernel(
-    order, x_h, c_h, wq_h, wkv_h, wo_h, wg_h, wu_h, wd_h, ga, gf, coarse, fine,
+    order, x_h, c_h, wq_h, wkv_h, wo_h, wg_h, wu_h, wd_h, ga_h, gf_h, coarse_h, fine_h,
     bo, gi, o_q, o_kv, o_o, o_g, o_u, o_d, gain_a, gain_f,
-    x, cot, wq, wkv, wo, wg, wu, wd, row_g, row_u, row_q, row_kv,
+    ga, gf, coarse, fine, x, cot, wq, wkv, wo, wg, wu, wd, row_g, row_u, row_q, row_kv,
     xn, kvall, kk, vv, kt, vt, qst, cos_t, sin_t, s_buf, pt, ob, rl,
-    zs, zr, mid, dmid, hn, da, bo_s, gi_s, dinner, act, act_p, g_first,
+    zs, z_near, z_far, mid, dmid, hn, da, bo_s, gi_s, dinner, act, act_p, down_first,
     xn_t, c_t, hn_t, xn_p, c_p, hn_p, da_p, ob_p, dqp, dqp_p, dkvp, dkvp_p,
     dkv_r, delta, r1f, r2f, r3f, r4f, r1a, r2a, r3a, r4a,
     g_q, g_kv, g_o, g_g, g_u, g_d, gain_s, gain_r,
@@ -109,6 +109,10 @@
             local_done.add(id(copy))
 
     x_load = copy_local(x_h, x)
+    table_loads = [
+        copy_local(ga_h, ga), copy_local(gf_h, gf),
+        copy_local(coarse_h, coarse), copy_local(fine_h, fine),
+    ]
     wkv_load = copy_local(wkv_h, wkv)
     wq_load = copy_local(wq_h, wq)
 
@@ -121,29 +125,41 @@
     for peer in greeted:
         pl.semaphore_signal(barrier, inc=1, device_id=peer, device_id_type=MESH)
 
-    sent = []
-    arrived, released = set(), set()
-
-    def send(src, dst, peer):
-        n = len(sent)
-        copy = pltpu.make_async_remote_copy(
-            src_ref=src, dst_ref=dst, send_sem=send_sem.at[n], recv_sem=recv_sem.at[n],
-            device_id=peer, device_id_type=MESH,
-        )
-        copy.start()
-        sent.append(copy)
-        return copy
-
-    def wait_recv(copies):
-        for copy in copies:
-            copy.wait_recv()
-            arrived.add(id(copy))
-
-    def wait_send(copies):
-        for copy in copies:
-            copy.wait_send()
-            released.add(id(copy))
-
+    groups = []
+
+    class Group:
+        def __init__(self, size):
+            self.n = len(groups)
+            self.size = size
+            self.arrived = self.released = self.used = False
+            groups.append(self)
+
+        def copy(self, src, dst, peer):
+            return pltpu.make_async_remote_copy(
+                src_ref=src, dst_ref=dst, send_sem=send_sem.at[self.n],
+                recv_sem=recv_sem.at[self.n], device_id=peer, device_id_type=MESH,
+            )
+
+        def send(self, src, dst, peer):
+            self.used = True
+            self.copy(src, dst, peer).start()
+
+        def wait_recv(self):
+            if self.used and not self.arrived:
+                self.copy(self.size, self.size, core_peer).wait_recv()
+                self.arrived = True
+
+        def wait_send(self):
+            if self.used and not self.released:
+                self.copy(self.size, self.size, core_peer).wait_send()
+                self.released = True
+
+    def send_one(src, dst, peer):
+        group = Group(dst)
+        group.send(src, dst, peer)
+        return group
+
+    wait_local(*table_loads)
     pick = lax.broadcasted_iota(jnp.int32, (16, 128), 0)
     sign = jnp.where(lane_of((BLOCK, 128)) % HD < HD // 2, -1.0, 1.0).astype(F32)
     for b in range(2):
@@ -176,7 +192,9 @@
     kvp = dot(normed, wkv[...])
     kvall[ictx] = jnp.where(low_lane, rot(kvp), kvp).astype(BF16)
     pl.semaphore_wait(barrier, len(greeted))
-    kv_copies = [send(kvall.at[ictx], kvall.at[ictx], ctx_peer(k)) for k in range(1, 8)]
+    kv_group = Group(kvall.at[pl.ds(0, 7)])
+    for k in (4, 5, 3, 2, 6, 7, 1):
+        kv_group.send(kvall.at[ictx], kvall.at[ictx], ctx_peer(k))
     wait_local(wq_load)
     wo_load = copy_local(wo_h, wo)
     wg_load = copy_local(wg_h, wg)
@@ -205,16 +223,17 @@
 
     turned = (4, 4, 2, 2, 32, T)
     xn_t[...] = normed.T.reshape(turned)
-    xnt_copy = send(xn_t.at[:, :, other], xn_p, core_peer)
+    xnt_copy = send_one(xn_t.at[:, :, other], xn_p, core_peer)
     wait_local(cot_load)
     cot_rows = cot[...]
     c_t[...] = cot_rows.T.reshape(turned)
-    ct_copy = send(c_t.at[:, :, other], c_p, core_peer)
+    ct_copy = send_one(c_t.at[:, :, other], c_p, core_peer)
     wait_local(wd_load)
     for s, n in tiles(FC, 512):
-        dinner[:, s : s + n] = dot_nt(cot_rows, wd[s : s + n, :])
-
-    wait_recv(kv_copies)
+        rows = slice(s // 128, (s + n) // 128)
+        dinner[:, s : s + n] = dot_nt(cot_rows, wd[rows].reshape(n, D))
+
+    kv_group.wait_recv()
     for j in range(8):
         wide = kvall[j].astype(F32)
         rolled = pltpu.roll(wide, HD, 1)
@@ -274,70 +293,107 @@
         return pl.ds(pl.multiple_of(TA + z * 16, 16), 16)
 
     kept = (slice(0, 32), slice(32, 48))
-    all_cols = pl.ds(0, D)
-
-    def z_scatter(src, n, part, cols=all_cols):
-        return [
-            send(
-                src.at[z_rows(part, (iz + k) % 4), cols], zr.at[n, k - 1, kept[part], cols],
-                z_peer(k),
-            )
-            for k in (2, 1, 3)
-        ]
-
-    def z_sum(src, n, part):
-        total = src[z_rows(part, iz), :].astype(F32)
-        for k in range(3):
-            total = total + zr[n, k, kept[part], :].astype(F32)
-        return total
-
-    def z_gather(buf, part, own=None):
-        rows = z_rows(part, iz)
-        src = buf.at[rows] if own is None else own.at[kept[part]]
-        return [send(src, buf.at[rows], z_peer(k)) for k in (2, 1, 3)]
+    cols_l, cols_r, all_cols = pl.ds(0, D // 2), pl.ds(D // 2, D // 2), pl.ds(0, D)
+    zp, zm, z2 = (iz + 1) % 4, (iz + 3) % 4, (iz + 2) % 4
+
+    class ZScatter:
+        def __init__(self, src, n, part):
+            self.src, self.n, self.part = src, n, part
+            self.far = Group(z_far.at[n, :, kept[part]])
+            self.near = Group(z_near.at[n, :, kept[part]])
+
+        def first(self, cols=(0, D // 2, D // 2)):
+            l, r, width = cols
+            src, n, part = self.src, self.n, self.part
+            keep = kept[part]
+            left, right = pl.ds(l, width), pl.ds(r, width)
+            if l is not None:
+                far = z_far.at[n, 0, keep, left]
+                self.far.send(src.at[z_rows(part, z2), left], far, z_peer(1))
+            if r is not None:
+                far = z_far.at[n, 1, keep, pl.ds(r - D // 2, width)]
+                self.far.send(src.at[z_rows(part, z2), right], far, z_peer(3))
+            if l is not None:
+                near = z_near.at[n, 1, keep, left]
+                self.near.send(src.at[z_rows(part, zm), left], near, z_peer(3))
+            if r is not None:
+                near = z_near.at[n, 0, keep, right]
+                self.near.send(src.at[z_rows(part, zp), right], near, z_peer(1))
+
+        def second(self):
+            src, n, part = self.src, self.n, self.part
+            keep = kept[part]
+            self.far.wait_recv()
+            for way, z, cols, k in ((0, zp, cols_l, 1), (1, zm, cols_r, 3)):
+                rows = z_rows(part, z)
+                total = src[rows, cols].astype(F32) + z_far[n, way, keep, :].astype(F32)
+                src[rows, cols] = total.astype(BF16)
+                self.near.send(src.at[rows, cols], z_near.at[n, way, keep, cols], z_peer(k))
+
+        def result(self):
+            self.near.wait_recv()
+            total = self.src[z_rows(self.part, iz), :].astype(F32)
+            for way in range(2):
+                total = total + z_near[self.n, way, kept[self.part], :].astype(F32)
+            return total
+
+        def wait_send(self):
+            self.far.wait_send()
+            self.near.wait_send()
+
+    class ZGather:
+        def __init__(self, buf, part, own=None):
+            self.buf, self.part = buf, part
+            self.far = Group(z_far.at[0, :, kept[part]])
+            self.near = Group(z_near.at[0, :, kept[part]])
+            rows = z_rows(part, iz)
+            for cols, way, k, group in (
+                (cols_l, 0, 1, self.far), (cols_r, 1, 3, self.far),
+                (cols_r, 0, 1, self.near), (cols_l, 1, 3, self.near),
+            ):
+                src = buf.at[rows, cols] if own is None else own.at[kept[part], cols]
+                group.send(src, buf.at[rows, cols], z_peer(k))
+
+        def second(self):
+            self.far.wait_recv()
+            for z, cols, k in ((zm, cols_l, 1), (zp, cols_r, 3)):
+                piece = self.buf.at[z_rows(self.part, z), cols]
+                self.near.send(piece, piece, z_peer(k))
+
+        def wait_recv(self):
+            self.near.wait_recv()
 
     def project_out(part):
         rows = slice(0, TA) if part == 0 else slice(TA, T)
-        copies = []
-        for s, n in tiles(D, 1024):
-            zs[rows, s : s + n] = dot(ob[rows, :], wo[:, s : s + n]).astype(BF16)
-            copies += z_scatter(zs, 0, part, pl.ds(s, n))
-        return copies
+        scatter = ZScatter(zs, 0, part)
+        for l in (0, 512):
+            for s in (l, l + D // 2):
+                zs[rows, s : s + 512] = dot(ob[rows, :], wo[:, s : s + 512]).astype(BF16)
+            scatter.first((l, l + D // 2, 512))
+        return scatter
 
     attend(0)
     attend(1)
     wait_local(wo_load)
-    attn_copies = [project_out(0)]
+    attn_sums = [project_out(0)]
     attend(2)
-    attn_copies.append(project_out(1))
-    ob_copy = send(ob, ob_p, core_peer)
-
-    hn_copies = []
-    for part in range(2):
-        wait_recv(attn_copies[part])
-        m = x[z_rows(part, iz), :].astype(F32) + z_sum(zs, 0, part)
+    attn_sums.append(project_out(1))
+    ob_copy = send_one(ob, ob_p, core_peer)
+
+    hn_parts = []
+
+    def norm(part):
+        m = x[z_rows(part, iz), :].astype(F32) + attn_sums[part].result()
         mid[kept[part], :] = m
         hn[z_rows(part, iz), :] = (m * inv_rms(m) * gf[...]).astype(BF16)
-        hn_copies += z_gather(hn, part)
-
-    wait_local(wg_load, wu_load)
-    wait_recv(hn_copies)
-    hidden = hn[...]
-    act_copies = [[], [], []]
-    for s, n in FF_TILES:
-        cols = slice(s, s + n)
-        g = dot(hidden, wg[:, :, :, :, :, cols].reshape(D, n))
-        u = dot(hidden, wu[:, :, :, :, :, cols].reshape(D, n))
-        sig = 1.0 / (1.0 + jnp.exp(-g))
-        a = g * sig
-        di = dinner[:, cols]
-        act[0, :, cols] = (a * u).astype(BF16)
-        act[1, :, cols] = (di * u * sig * (1.0 + g * (1.0 - sig))).astype(BF16)
-        act[2, :, cols] = (di * a).astype(BF16)
-        for i in range(3):
-            act_copies[i].append(
-                send(act.at[i, :, pl.ds(s, n)], act_p.at[i, :, pl.ds(s, n)], core_peer)
-            )
+        hn_parts.append(ZGather(hn, part))
+
+    attn_sums[0].second()
+    attn_sums[1].second()
+    norm(0)
+    norm(1)
+    hn_parts[0].second()
+    hn_parts[1].second()
 
     xp, xm, x2 = (ix + 1) % 4, (ix + 3) % 4, (ix + 2) % 4
     yp, ym, y2 = (iy + 1) % 4, (iy + 3) % 4, (iy + 2) % 4
@@ -352,22 +408,24 @@
     first_rows = [(all4, x2, 0), (y2, all4, 1)]
     other_rows = [(all4, dx, 0) for dx in (xp, xm, ix)] + [(dy, all4, 1) for dy in (yp, ym, iy)]
 
-    def weight_grad(part, which, own_t, partner_t, own_b, partner_b, store=None, c0=0, n=None):
+    def weight_grad(part, which, own_t, partner_t, own_b, partner_b, b0=0, n=None, shift=0):
         ref, half, part_c0, part_n, _, _ = parts[part]
         n = part_n if n is None else n
+        early = which is first_rows and part < 3
         get_own, get_partner = own_part(own_t), partner_part(partner_t)
         a_own = jnp.concatenate([get_own(*i).reshape(128, T) for i in which], 0)
         a_partner = jnp.concatenate([get_partner(*i).reshape(128, T) for i in which], 0)
         for s, w in tiles(n, 256):
+            s = s + b0
             r = dot(a_own, own_b[:, s : s + w]) + dot(a_partner, partner_b[:, s : s + w])
             r = r.astype(BF16)
-            cols = slice(part_c0 + c0 + s, part_c0 + c0 + s + w)
+            cols = slice(part_c0 + shift + s, part_c0 + shift + s + w)
             for i, (dy, dx, h) in enumerate(which):
                 rows = r[i * 128 : (i + 1) * 128].reshape(4, 32, w)
-                if store is None:
+                if early:
+                    g_first[part][i, :, :, cols] = rows
+                else:
                     ref[half, dy, dx, h, :, cols] = rows
-                else:
-                    store[i, :, :, cols] = rows
 
     f_bufs = [[r.at[i] for r in (r1f, r2f, r3f, r4f)] for i in range(3)]
     a_bufs = [r1a, r2a, r3a, r4a]
@@ -378,6 +436,7 @@
         (wu, 1, 0, 512, a_bufs, 0),
         (wu, 1, 512, 640, a_bufs, 512),
     ]
+    g_first = [down_first.at[0:2], wd.at[0:2], wd.at[2:4]]
     flights = {}
     lo2, hi2 = pl.ds(0, 2), pl.ds(2, 2)
     all32, lo16, hi16 = pl.ds(0, 32), pl.ds(0, 16), pl.ds(16, 16)
@@ -386,18 +445,20 @@
         ref, half, c0, n, _, _ = parts[part]
         return (half, dy, dx, h, all32 if rows is None else rows, pl.ds(c0, n))
 
-    def outgoing(part, step):
-        if step == 0 and part == 0:
-            return (
-                (g_first.at[0, lo2], g_first.at[0, hi2]),
-                (g_first.at[1, lo2], g_first.at[1, hi2]),
+    def first_piece(part, flow, pair, s, n):
+        if part < 3:
+            return g_first[part].at[flow, pair, :, pl.ds(s, n)]
+        ref, half, c0, _, _, _ = parts[part]
+        dy, dx = (pair, x2) if flow == 0 else (y2, pair)
+        return ref.at[half, dy, dx, flow, :, pl.ds(c0 + s, n)]
+
+    def outgoing(part, step, s, n):
+        if step == 0:
+            return tuple(
+                tuple(first_piece(part, flow, pair, s, n) for pair in (lo2, hi2))
+                for flow in range(2)
             )
-        if step == 0:
-            index = (
-                (g_index(part, lo2, x2, 0), g_index(part, hi2, x2, 0)),
-                (g_index(part, y2, lo2, 1), g_index(part, y2, hi2, 1)),
-            )
-        elif step == 1:
+        if step == 1:
             index = (
                 (g_index(part, all4, xp, 0), g_index(part, all4, xm, 0)),
                 (g_index(part, yp, all4, 1), g_index(part, ym, all4, 1)),
@@ -415,19 +476,22 @@
         ref = parts[part][0]
         return tuple(tuple(ref.at[i] for i in flow) for flow in index)
 
-    def landing(part, step, flow, way):
-        _, _, _, n, bufs, b0 = parts[part]
-        return bufs[step].at[flow, way, ..., pl.ds(b0, n)]
-
-    def rs_send(part, step):
-        out = outgoing(part, step)
+    def landing(part, step, flow, way, s=0, n=None):
+        _, _, _, part_n, bufs, b0 = parts[part]
+        return bufs[step].at[flow, way, ..., pl.ds(b0 + s, part_n if n is None else n)]
+
+    def rs_send(part, step, s=0, n=None):
+        _, _, _, part_n, bufs, b0 = parts[part]
+        n = part_n if n is None else n
+        out = outgoing(part, step, s, n)
+        if (part, step) not in flights:
+            flights[part, step] = Group(bufs[step].at[..., pl.ds(b0, part_n)])
+        group = flights[part, step]
         for flow in range(2):
             along_x = (flow == 0) == (step < 2)
             for way, k in ((0, 1), (1, 3)):
                 peer = x_peer(k) if along_x else y_peer(k)
-                flights[part, step, flow, way] = send(
-                    out[flow][way], landing(part, step, flow, way), peer
-                )
+                group.send(out[flow][way], landing(part, step, flow, way, s, n), peer)
 
     def add_in(ref, index, *arrived):
         total = ref[index].astype(F32)
@@ -437,8 +501,8 @@
 
     def rs_recv(part, step):
         ref = parts[part][0]
+        flights[part, step].wait_recv()
         for flow in range(2):
-            wait_recv([flights[part, step, flow, way] for way in range(2)])
             got = [landing(part, step, flow, way) for way in range(2)]
             if step == 0:
                 if flow == 0:
@@ -476,58 +540,96 @@
         for stage, out, s, n in outs:
             copy_local(stage, out)
 
+    wait_local(wg_load, wu_load)
+    for part in hn_parts:
+        part.wait_recv()
+    hidden = hn[...]
+    inner_groups = [Group(act_p.at[0, :, pl.ds(s, n)]) for s, n in FF_TILES]
+    act_groups = [None, Group(act_p.at[1]), Group(act_p.at[2])]
+
+    def first_of_down(i):
+        s, n = FF_TILES[i]
+        inner_groups[i].wait_recv()
+        weight_grad(0, first_rows, c_t, c_p, act.at[0], act_p.at[0], s, n)
+        rs_send(0, 0, s, n)
+
+    ct_copy.wait_recv()
+    for t, (s, n) in enumerate(FF_TILES):
+        cols = slice(s, s + n)
+        g = dot(hidden, wg[:, :, :, :, :, cols].reshape(D, n))
+        u = dot(hidden, wu[:, :, :, :, :, cols].reshape(D, n))
+        sig = 1.0 / (1.0 + jnp.exp(-g))
+        a = g * sig
+        di = dinner[:, cols]
+        act[0, :, cols] = (a * u).astype(BF16)
+        piece = pl.ds(s, n)
+        inner_groups[t].send(act.at[0, :, piece], act_p.at[0, :, piece], core_peer)
+        act[1, :, cols] = (di * u * sig * (1.0 + g * (1.0 - sig))).astype(BF16)
+        act[2, :, cols] = (di * a).astype(BF16)
+        for i in (1, 2):
+            act_groups[i].send(act.at[i, :, piece], act_p.at[i, :, piece], core_peer)
+        if t > 0:
+            first_of_down(t - 1)
     hn_t[...] = hidden.T.reshape(turned)
-    hnt_copy = send(hn_t.at[:, :, other], hn_p, core_peer)
-    wait_recv([ct_copy] + act_copies[0])
-    weight_grad(0, first_rows, c_t, c_p, act.at[0], act_p.at[0], store=g_first)
-    rs_send(0, 0)
-
-    wait_send([copy for copies in attn_copies for copy in copies])
-    dhn_copies = [[], []]
-    for t in range(4):
+    hnt_copy = send_one(hn_t.at[:, :, other], hn_p, core_peer)
+    first_of_down(3)
+    inner = act[0]
+    for s, n in tiles(D, 512):
+        xn[:, s : s + n] = dot(inner, wd[..., s : s + n].reshape(FC, n)).astype(BF16)
+    hnt_copy.wait_recv()
+    act_groups[1].wait_recv()
+    weight_grad(1, first_rows, hn_t, hn_p, act.at[1], act_p.at[1])
+    rs_send(1, 0)
+
+    for scatter in attn_sums:
+        scatter.wait_send()
+    dhn_sums = [ZScatter(zs, 1, part) for part in range(2)]
+    for t in (0, 2, 1, 3):
         cols = slice(t * 512, (t + 1) * 512)
         block = (t // 2, slice((t % 2) * 2, (t % 2) * 2 + 2))
         r = dot_nt(act[1], wg[block].reshape(512, FC)) + dot_nt(act[2], wu[block].reshape(512, FC))
         zs[:, cols] = r.astype(BF16)
-        dhn_copies[0] += z_scatter(zs, 1, 0, pl.ds(t * 512, 512))
-    dhn_copies[1] += z_scatter(zs, 1, 1)
-    wait_recv([hnt_copy] + act_copies[1])
-    weight_grad(1, first_rows, hn_t, hn_p, act.at[1], act_p.at[1])
-    rs_send(1, 0)
-    wait_recv(act_copies[2])
-    weight_grad(2, first_rows, hn_t, hn_p, act.at[2], act_p.at[2])
-    rs_send(2, 0)
+        dhn_sums[0].first((t * 512, None, 512) if t < 2 else (None, t * 512, 512))
+        if t == 2:
+            act_groups[2].wait_recv()
+            weight_grad(2, first_rows, hn_t, hn_p, act.at[2], act_p.at[2])
+            rs_send(2, 0)
+    dhn_sums[1].first()
     weight_grad(0, other_rows, c_t, c_p, act.at[0], act_p.at[0])
     rs_turn(0, 0)
-
-    da_copies = []
+    dhn_sums[0].second()
+    dhn_sums[1].second()
+    weight_grad(1, other_rows, hn_t, hn_p, act.at[1], act_p.at[1])
+    weight_grad(2, other_rows, hn_t, hn_p, act.at[2], act_p.at[2])
+
+    da_parts = []
 
     def norm_back(part):
-        wait_recv(dhn_copies[part])
         m = mid[kept[part], :]
         r2 = inv_rms(m)
         mhat = m * r2
-        scaled = z_sum(zs, 1, part) * gf[...]
+        scaled = dhn_sums[part].result() * gf[...]
         rows = z_rows(part, iz)
         dm = cot[rows, :].astype(F32) + r2 * (
             scaled - mhat * jnp.mean(scaled * mhat, -1, keepdims=True)
         )
         dmid[kept[part], :] = dm
         da[rows, :] = dm.astype(BF16)
-        da_copies.extend(z_gather(da, part))
+        da_parts.append(ZGather(da, part))
 
     norm_back(0)
-    weight_grad(1, other_rows, hn_t, hn_p, act.at[1], act_p.at[1])
     norm_back(1)
-    weight_grad(2, other_rows, hn_t, hn_p, act.at[2], act_p.at[2])
     rs_turn(1, 0)
-    inner = act[0]
-    for s, n in tiles(D, 512):
-        xn[:, s : s + n] = dot(inner, wd[:, s : s + n]).astype(BF16)
+    da_parts[0].second()
+    da_parts[1].second()
     rs_turn(2, 0)
-
-    wait_recv(da_copies)
-    ffn_copies = [z_scatter(xn, 2, part) for part in range(2)]
+    rs_turn(0, 1)
+
+    for part in da_parts:
+        part.wait_recv()
+    ffn_sums = [ZScatter(xn, 2, part) for part in range(2)]
+    for scatter in ffn_sums:
+        scatter.first()
     grad_attn = da[...]
     for s, n in tiles(QC, 256):
         grad_rows = dot_nt(grad_attn, wo[s : s + n, :])
@@ -542,13 +644,13 @@
                 sums = jnp.sum(by_row[i * HD : (i + 1) * HD], 0, keepdims=True)
                 delta[:, h * TA : (h + 1) * TA] = sums[:, 0:TA]
                 delta[:, 8 * TA + h * 64 : 8 * TA + (h + 1) * 64] = sums[:, TA:T]
-    wait_send([ct_copy])
+    ct_copy.wait_send()
     c_t[...] = grad_attn.T.reshape(turned)
-    dat_copy = send(c_t.at[:, :, other], da_p, core_peer)
+    dat_copy = send_one(c_t.at[:, :, other], da_p, core_peer)
     dob = kk
 
-    wait_send(kv_copies)
-    dkv_copies = []
+    kv_group.wait_send()
+    dkv_group = Group(kvall.at[pl.ds(0, 7)])
     for i, step in enumerate((2, 1, 3, 0)):
         chip = (ix + step) % 4
         rows = pl.ds(pl.multiple_of(chip * CHIP_KEYS, CHIP_KEYS), CHIP_KEYS)
@@ -568,13 +670,10 @@
             kvall[chip * 2 + c] = both[c * T : (c + 1) * T]
         for c, goal in ((0, core), (1, other)):
             if step != 0 or c == 1:
-                dkv_copies.append(
-                    send(kvall.at[chip * 2 + goal], dkv_r.at[i, c], (iy, chip * 2 + goal, iz))
-                )
+                dkv_group.send(kvall.at[chip * 2 + goal], dkv_r.at[i, c], (iy, chip * 2 + goal, iz))
         if i == 1:
-            wait_recv([dat_copy, ob_copy])
-            weight_grad(3, first_rows, c_t, da_p, ob, ob_p)
-            rs_send(3, 0)
+            for scatter in ffn_sums:
+                scatter.second()
     dq_t = dot(kt[...], pt[...]) * (HD ** -0.5)
     for p in range(PAIRS):
         a0 = dq_t[:, p * 256 : p * 256 + 128].T
@@ -584,72 +683,82 @@
             [jnp.where(low_a, a0, a1), jnp.where(low_b, b[0:64], b[64:128])], 0
         )
         dqp[:, p * 128 : (p + 1) * 128] = rot_back(dq).astype(BF16)
-    dqp_copy = send(dqp, dqp_p, core_peer)
-
-    wait_recv(dkv_copies)
+    dqp_copy = send_one(dqp, dqp_p, core_peer)
+
+    bo_parts = []
+    for part in range(2):
+        bo_s[kept[part], :] = (mid[kept[part], :] + ffn_sums[part].result()).astype(BF16)
+        copy_local(bo_s.at[kept[part]], bo.at[z_rows(part, iz)])
+        bo_parts.append(ZGather(bo, part, bo_s))
+    dat_copy.wait_recv()
+    ob_copy.wait_recv()
+    weight_grad(3, first_rows, c_t, da_p, ob, ob_p)
+    rs_send(3, 0)
+    weight_grad(3, other_rows, c_t, da_p, ob, ob_p)
+    rs_turn(1, 1)
+
+    dkv_group.wait_recv()
     home = kvall[ictx].astype(F32) + dkv_r[3, 1].astype(F32)
     for i in range(3):
         for c in range(2):
             home = home + dkv_r[i, c].astype(F32)
     dkvp[...] = jnp.where(low_lane, rot_back(home), home).astype(BF16)
-    dkvp_copy = send(dkvp, dkvp_p, core_peer)
-    wait_send([copy for copies in dhn_copies for copy in copies])
+    dkvp_copy = send_one(dkvp, dkvp_p, core_peer)
+    for scatter in dhn_sums:
+        scatter.wait_send()
     q_rows, kv_rows = dqp[...], dkvp[...]
-    dxn_copies = [[], []]
-    for s, n in tiles(D, 512):
-        r = dot_nt(q_rows, wq[s : s + n, :]) + dot_nt(kv_rows, wkv[s : s + n, :])
-        zs[:, s : s + n] = r.astype(BF16)
-        dxn_copies[0] += z_scatter(zs, 3, 0, pl.ds(s, n))
-    dxn_copies[1] += z_scatter(zs, 3, 1)
-
-    wait_recv([xnt_copy, dqp_copy])
-    weight_grad(4, first_rows, xn_t, xn_p, dqp, dqp_p, c0=0, n=512)
-    wait_recv([dkvp_copy])
-    weight_grad(4, first_rows, xn_t, xn_p, dkvp, dkvp_p, c0=512, n=128)
+    dxn_sums = [ZScatter(zs, 3, part) for part in range(2)]
+    for l in (0, 512):
+        for s in (l, l + D // 2):
+            cols = slice(s, s + 512)
+            r = dot_nt(q_rows, wq[cols, :]) + dot_nt(kv_rows, wkv[cols, :])
+            zs[:, cols] = r.astype(BF16)
+        dxn_sums[0].first((l, l + D // 2, 512))
+    dxn_sums[1].first()
+
+    for part in bo_parts:
+        part.second()
+    xnt_copy.wait_recv()
+    dqp_copy.wait_recv()
+    weight_grad(4, first_rows, xn_t, xn_p, dqp, dqp_p, n=512)
+    dkvp_copy.wait_recv()
+    weight_grad(4, first_rows, xn_t, xn_p, dkvp, dkvp_p, n=128, shift=512)
     rs_send(4, 0)
-    rs_turn(0, 1)
-    weight_grad(3, other_rows, c_t, da_p, ob, ob_p)
-    weight_grad(4, other_rows, xn_t, xn_p, dqp, dqp_p, c0=0, n=512)
-    weight_grad(4, other_rows, xn_t, xn_p, dkvp, dkvp_p, c0=512, n=128)
-    rs_turn(1, 1)
-
-    own_rows_out = []
-    bo_copies = []
-    for part in range(2):
-        wait_recv(ffn_copies[part])
-        bo_s[kept[part], :] = (mid[kept[part], :] + z_sum(xn, 2, part)).astype(BF16)
-        copy_local(bo_s.at[kept[part]], bo.at[z_rows(part, iz)])
-        bo_copies += z_gather(bo, part, bo_s)
-
+    dxn_sums[0].second()
+    dxn_sums[1].second()
+    weight_grad(4, other_rows, xn_t, xn_p, dqp, dqp_p, n=512)
+    weight_grad(4, other_rows, xn_t, xn_p, dkvp, dkvp_p, n=128, shift=512)
     rs_turn(3, 0)
-    rs_turn(4, 0)
-
-    for part in range(2):
-        wait_recv(dxn_copies[part])
+
+    gi_parts = []
+
+    def first_norm_back(part):
         rows = x[z_rows(part, iz), :].astype(F32)
         r1 = inv_rms(rows)
         xhat = rows * r1
-        scaled = z_sum(zs, 3, part) * ga[...]
+        scaled = dxn_sums[part].result() * ga[...]
         gi_s[kept[part], :] = (
             dmid[kept[part], :]
             + r1 * (scaled - xhat * jnp.mean(scaled * xhat, -1, keepdims=True))
         ).astype(BF16)
         copy_local(gi_s.at[kept[part]], gi.at[z_rows(part, iz)])
-        z_gather(gi, part, gi_s)
-
+        gi_parts.append(ZGather(gi, part, gi_s))
+
+    rs_turn(4, 0)
     rs_turn(2, 1)
+    first_norm_back(0)
+    first_norm_back(1)
+    rs_turn(1, 2)
+    rs_turn(4, 1)
+    gi_parts[0].second()
+    gi_parts[1].second()
+    rs_turn(2, 2)
+    rs_turn(3, 1)
     rs_turn(0, 2)
-    rs_turn(1, 2)
-    rs_turn(3, 1)
-    rs_turn(4, 1)
-    rs_turn(2, 2)
-    rs_last(0, [(g_d, o_d, 0, FC)])
+    rs_turn(4, 2)
     rs_last(1, [(g_g, o_g, 0, FC)])
     rs_turn(3, 2)
-    rs_turn(4, 2)
     rs_last(2, [(g_u, o_u, 0, FC)])
-    rs_last(3, [(g_o, o_o, 0, 512)])
-    rs_last(4, [(g_q, o_q, 0, 512), (g_kv, o_kv, 512, 128)])
 
     wait_local(*row_loads)
 
@@ -662,25 +771,38 @@
                 total = total + grad[:, s : s + 128] * w[:, s : s + 128].astype(F32)
         return jnp.sum(total.T, 0, keepdims=True)
 
-    gain_s[...] = jnp.zeros((8, 128), F32)
-    gain_s[0:1, 0:64] = row_products([(g_g, row_g), (g_u, row_u)])
-    gain_s[1:2, 0:64] = row_products([(g_q, row_q), (g_kv, row_kv)])
-    gain_copies = [send(gain_s, gain_r.at[k - 1], z_peer(k)) for k in range(1, 4)]
-    wait_recv(gain_copies)
-    total = gain_s[...]
-    for k in range(3):
-        total = total + gain_r[k]
+    def exchange_gain(i, pairs):
+        gain_s[i] = jnp.broadcast_to(row_products(pairs), (8, 64))
+        group = Group(gain_r.at[i])
+        for k in range(1, 4):
+            group.send(gain_s.at[i], gain_r.at[i, k - 1], z_peer(k))
+        return group
+
+    def gain_total(i, group):
+        group.wait_recv()
+        total = gain_s[i]
+        for k in range(3):
+            total = total + gain_r[i, k]
+        return total[0:1]
+
+    gain_f_group = exchange_gain(0, [(g_g, row_g), (g_u, row_u)])
+    rs_last(4, [(g_q, o_q, 0, 512), (g_kv, o_kv, 512, 128)])
+    gain_a_group = exchange_gain(1, [(g_q, row_q), (g_kv, row_kv)])
+    rs_last(0, [(g_d, o_d, 0, FC)])
+    rs_last(3, [(g_o, o_o, 0, 512)])
     chip_cols = pl.ds(pl.multiple_of((iy * 4 + ix) * 128, 128), 128)
 
     def own_gain(ref):
         v = ref[:, chip_cols]
         return jnp.where(core == 1, pltpu.roll(v, 64, 1), v)[:, 0:64]
 
-    gain_f[...] = total[0:1, 0:64] / own_gain(gf)
-    gain_a[...] = total[1:2, 0:64] / own_gain(ga)
-
-    wait_recv([copy for copy in sent if id(copy) not in arrived])
-    wait_send([copy for copy in sent if id(copy) not in released])
+    gain_f[...] = gain_total(0, gain_f_group) / own_gain(gf)
+    gain_a[...] = gain_total(1, gain_a_group) / own_gain(ga)
+
+    for group in groups:
+        group.wait_recv()
+    for group in groups:
+        group.wait_send()
     wait_local(*[copy for copy in local if id(copy) not in local_done])
 
 
@@ -715,8 +837,8 @@
         copy.wait()
 
 
-N_SENDS = 224
-N_LOCAL = 40
+N_GROUPS = 76
+N_LOCAL = 32
 
 
 def per_device(
@@ -734,9 +856,10 @@
     scratch = [
         pltpu.VMEM(s, t)
         for s, t in (
+            ((1, D), F32), ((1, D), F32), ((2, 16, 128), F32), ((2, BLOCK, 128), F32),
             ((T, D), BF16), ((T, D), BF16),
             ((D, QC), BF16), ((D, 128), BF16), ((QC, D), BF16),
-            (wide, BF16), (wide, BF16), ((FC, D), BF16),
+            (wide, BF16), (wide, BF16), ((11, 4, 32, D), BF16),
             ((2, 32, FC), BF16), ((2, 32, FC), BF16), ((64, QC), BF16), ((64, 128), BF16),
             ((T, D), BF16), ((8, T, 128), BF16),
             ((KEYS, 128), BF16), ((KEYS, 128), BF16),
@@ -744,7 +867,7 @@
             ((QUERIES, 128), BF16), ((T, 128), F32), ((T, 128), F32),
             ((KEYS, CHUNK), F32), ((KEYS, QUERIES), BF16),
             ((T, QC), BF16), ((T, QC), F32),
-            ((T, D), BF16), ((4, 3, R, D), BF16),
+            ((T, D), BF16), ((4, 2, R, D), BF16), ((4, 2, R, D // 2), BF16),
             ((R, D), F32), ((R, D), F32),
             ((T, D), BF16), ((T, D), BF16), ((R, D), BF16), ((R, D), BF16),
             ((T, FC), F32), ((3, T, FC), BF16), ((3, T, FC), BF16),
@@ -760,12 +883,12 @@
             ((2, 2, 16, 1152), BF16), ((2, 2, 32, 1152), BF16),
             ((64, QC), F32), ((64, 128), F32), ((64, QC), F32),
             ((64, FC), F32), ((64, FC), F32), ((64, FC), F32),
-            ((8, 128), F32), ((3, 8, 128), F32),
+            ((2, 8, 64), F32), ((2, 3, 8, 64), F32),
         )
     ] + [
         pltpu.SemaphoreType.DMA((N_LOCAL,)),
-        pltpu.SemaphoreType.DMA((N_SENDS,)),
-        pltpu.SemaphoreType.DMA((N_SENDS,)),
+        pltpu.SemaphoreType.DMA((N_GROUPS,)),
+        pltpu.SemaphoreType.DMA((N_GROUPS,)),
     ]
     grads = (
         shape((64, QC), F32), shape((64, 128), F32), shape((64, QC), F32),
@@ -775,7 +898,7 @@
     outs = pl.pallas_call(
         layer_kernel,
         out_shape=(shape((T, D), BF16), shape((T, D), BF16)) + grads,
-        in_specs=[smem] + [any_spec] * 8 + [vmem] * 4,
+        in_specs=[smem] + [any_spec] * 12,
         out_specs=(any_spec,) * 8 + (vmem,) * 2,
         scratch_shapes=scratch,
         compiler_params=pltpu.CompilerParams(
@@ -783,7 +906,8 @@
         ),
     )(
         block_order, hidden_in.reshape(T, D), cotangent.reshape(T, D),
-        w_query, w_keyval, w_output, w_gate.reshape(wide), w_up.reshape(wide), w_down,
+        w_query, w_keyval, w_output, w_gate.reshape(wide), w_up.reshape(wide),
+        w_down.reshape(11, 4, 32, D),
         gain_attn.reshape(1, D), gain_ffn.reshape(1, D), coarse, fine,
     )
     outs = pl.pallas_call(

time: 126 us -> 119 us (0.944)
  Pallas kernels: 125 us -> 118 us
    pallas_call x1, Pallas kernels: 122 us -> 115 us  [per_device(): pl.pallas_call(layer_kernel, out_shape=(shape((T, D), BF16), shape((T, D)...]
where the time goes in v3:
time: 119 us
  Pallas kernels  118 us (99%)
    pallas_call x1, Pallas kernels, per_device(): pl.pallas_call(layer_kernel, out_shape=(shape((T, D), BF16), shape((T, D)...  115 us
    pallas_call x1, Pallas kernels, per_device(): pl.pallas_call(store_kernel, out_shape=(shape((T, D), BF16), shape((T, D)...  3.09 us

profile of v3, /device:TPU:0, one launch (start us, length us, event | category | flops | bytes accessed | tf_op | source)
XLA Modules:
  0.0 118.6 jit_solution(11536097593379967611)
XLA Ops:
  0.6 114.7 %shard_map.204 = (bf16[192,2048]{1,0:T(8,128)(2,1)}, bf16[192,2048]{1,0:T(8,128)(2,1)}, f32[64,512]{1,0:T(8,128)}, f32[64,128]{1,0:T(8,128)}, f32[64,512]{1,0:T(...) custom-call(s32[1,16]{1,0:T(1,128)} %order.1, ...), custom_call_target="tpu_custom_call" | custom-call | tf_op jit(solution)/shard_map/pallas_call | solution.py:898
  115.3 3.1 %shard_map.205 = (bf16[192,2048]{1,0:T(8,128)(2,1)}, f32[192,2048]{1,0:T(8,128)}, f32[64,512]{1,0:T(8,128)}, f32[64,128]{1,0:T(8,128)}, f32[64,512]{1,0:T(8,128)...) custom-call(bf16[192,2048]{1,0:T(8,128)(2,1)} %get-tuple-element.30.r, ...), custom_call_target="tpu_custom_call" | custom-call | tf_op jit(solution)/shard_map/pallas_call | solution.py:913

commit v4 on v3

--- a/solution.py
+++ b/solution.py
@@ -67,12 +67,16 @@
     bo, gi, o_q, o_kv, o_o, o_g, o_u, o_d, gain_a, gain_f,
     ga, gf, coarse, fine, x, cot, wq, wkv, wo, wg, wu, wd, row_g, row_u, row_q, row_kv,
     xn, kvall, kk, vv, kt, vt, qst, cos_t, sin_t, s_buf, pt, ob, rl,
-    zs, z_near, z_far, mid, dmid, hn, da, bo_s, gi_s, dinner, act, act_p, down_first,
+    zs, z_near, z_far, mid, dmid, hn, da, bo_s, gi_s, dinner, act, act_p, g_first,
     xn_t, c_t, hn_t, xn_p, c_p, hn_p, da_p, ob_p, dqp, dqp_p, dkvp, dkvp_p,
     dkv_r, delta, r1f, r2f, r3f, r4f, r1a, r2a, r3a, r4a,
-    g_q, g_kv, g_o, g_g, g_u, g_d, gain_s, gain_r,
+    gain_s, gain_r,
     local_sem, send_sem, recv_sem,
 ):
+    g_g, g_u, g_d = (dinner.at[i * 64 : (i + 1) * 64] for i in range(3))
+    g_q, g_o, g_kv = (s_buf.at[i * 64 : (i + 1) * 64] for i in range(3))
+    g_kv = g_kv.at[:, 0:128]
+
     iy = lax.axis_index("dp")
     ictx = lax.axis_index("ctx")
     iz = lax.axis_index("tensor")
@@ -408,7 +412,7 @@
     first_rows = [(all4, x2, 0), (y2, all4, 1)]
     other_rows = [(all4, dx, 0) for dx in (xp, xm, ix)] + [(dy, all4, 1) for dy in (yp, ym, iy)]
 
-    def weight_grad(part, which, own_t, partner_t, own_b, partner_b, b0=0, n=None, shift=0):
+    def weight_grad(part, which, own_t, partner_t, own_b, partner_b, b0=0, n=None):
         ref, half, part_c0, part_n, _, _ = parts[part]
         n = part_n if n is None else n
         early = which is first_rows and part < 3
@@ -419,11 +423,11 @@
             s = s + b0
             r = dot(a_own, own_b[:, s : s + w]) + dot(a_partner, partner_b[:, s : s + w])
             r = r.astype(BF16)
-            cols = slice(part_c0 + shift + s, part_c0 + shift + s + w)
+            cols = slice(part_c0 + s, part_c0 + s + w)
             for i, (dy, dx, h) in enumerate(which):
                 rows = r[i * 128 : (i + 1) * 128].reshape(4, 32, w)
                 if early:
-                    g_first[part][i, :, :, cols] = rows
+                    g_first[part, i, :, :, cols] = rows
                 else:
                     ref[half, dy, dx, h, :, cols] = rows
 
@@ -434,9 +438,9 @@
         (wg, 0, 0, FC, f_bufs[1], 0),
         (wu, 0, 0, FC, f_bufs[2], 0),
         (wu, 1, 0, 512, a_bufs, 0),
-        (wu, 1, 512, 640, a_bufs, 512),
+        (wu, 1, 512, 512, a_bufs, 512),
+        (wu, 1, 1024, 128, a_bufs, 1024),
     ]
-    g_first = [down_first.at[0:2], wd.at[0:2], wd.at[2:4]]
     flights = {}
     lo2, hi2 = pl.ds(0, 2), pl.ds(2, 2)
     all32, lo16, hi16 = pl.ds(0, 32), pl.ds(0, 16), pl.ds(16, 16)
@@ -447,7 +451,7 @@
 
     def first_piece(part, flow, pair, s, n):
         if part < 3:
-            return g_first[part].at[flow, pair, :, pl.ds(s, n)]
+            return g_first.at[part, flow, pair, :, pl.ds(s, n)]
         ref, half, c0, _, _, _ = parts[part]
         dy, dx = (pair, x2) if flow == 0 else (y2, pair)
         return ref.at[half, dy, dx, flow, :, pl.ds(c0 + s, n)]
@@ -480,14 +484,14 @@
         _, _, _, part_n, bufs, b0 = parts[part]
         return bufs[step].at[flow, way, ..., pl.ds(b0 + s, part_n if n is None else n)]
 
-    def rs_send(part, step, s=0, n=None):
+    def rs_send(part, step, s=0, n=None, flows=(0, 1)):
         _, _, _, part_n, bufs, b0 = parts[part]
         n = part_n if n is None else n
         out = outgoing(part, step, s, n)
-        if (part, step) not in flights:
-            flights[part, step] = Group(bufs[step].at[..., pl.ds(b0, part_n)])
-        group = flights[part, step]
-        for flow in range(2):
+        for flow in flows:
+            if (part, step, flow) not in flights:
+                flights[part, step, flow] = Group(bufs[step].at[flow, ..., pl.ds(b0, part_n)])
+            group = flights[part, step, flow]
             along_x = (flow == 0) == (step < 2)
             for way, k in ((0, 1), (1, 3)):
                 peer = x_peer(k) if along_x else y_peer(k)
@@ -499,10 +503,10 @@
             total = total + a[...].astype(F32)
         ref[index] = total.astype(BF16)
 
-    def rs_recv(part, step):
+    def rs_recv(part, step, flows=(0, 1)):
         ref = parts[part][0]
-        flights[part, step].wait_recv()
-        for flow in range(2):
+        for flow in flows:
+            flights[part, step, flow].wait_recv()
             got = [landing(part, step, flow, way) for way in range(2)]
             if step == 0:
                 if flow == 0:
@@ -524,9 +528,10 @@
                     add_in(ref, g_index(part, iy, xp, 1, lo16), got[0])
                     add_in(ref, g_index(part, iy, xm, 1, hi16), got[1])
 
-    def rs_turn(part, step):
-        rs_recv(part, step)
-        rs_send(part, step + 1)
+    def rs_turn(part, step, flows=(0, 1)):
+        for flow in flows:
+            rs_recv(part, step, (flow,))
+            rs_send(part, step + 1, flows=(flow,))
 
     def rs_last(part, outs):
         rs_recv(part, 3)
@@ -544,16 +549,17 @@
     for part in hn_parts:
         part.wait_recv()
     hidden = hn[...]
-    inner_groups = [Group(act_p.at[0, :, pl.ds(s, n)]) for s, n in FF_TILES]
-    act_groups = [None, Group(act_p.at[1]), Group(act_p.at[2])]
-
-    def first_of_down(i):
-        s, n = FF_TILES[i]
-        inner_groups[i].wait_recv()
-        weight_grad(0, first_rows, c_t, c_p, act.at[0], act_p.at[0], s, n)
-        rs_send(0, 0, s, n)
-
-    ct_copy.wait_recv()
+    hn_t[...] = hidden.T.reshape(turned)
+    hnt_copy = send_one(hn_t.at[:, :, other], hn_p, core_peer)
+    act_groups = [Group(act_p.at[:, :, pl.ds(s, n)]) for s, n in FF_TILES]
+
+    def first_of_tile(t):
+        s, n = FF_TILES[t]
+        act_groups[t].wait_recv()
+        for part, own_t, partner_t in ((0, c_t, c_p), (1, hn_t, hn_p), (2, hn_t, hn_p)):
+            weight_grad(part, first_rows, own_t, partner_t, act.at[part], act_p.at[part], s, n)
+            rs_send(part, 0, s, n)
+
     for t, (s, n) in enumerate(FF_TILES):
         cols = slice(s, s + n)
         g = dot(hidden, wg[:, :, :, :, :, cols].reshape(D, n))
@@ -562,24 +568,15 @@
         a = g * sig
         di = dinner[:, cols]
         act[0, :, cols] = (a * u).astype(BF16)
-        piece = pl.ds(s, n)
-        inner_groups[t].send(act.at[0, :, piece], act_p.at[0, :, piece], core_peer)
         act[1, :, cols] = (di * u * sig * (1.0 + g * (1.0 - sig))).astype(BF16)
         act[2, :, cols] = (di * a).astype(BF16)
-        for i in (1, 2):
-            act_groups[i].send(act.at[i, :, piece], act_p.at[i, :, piece], core_peer)
-        if t > 0:
-            first_of_down(t - 1)
-    hn_t[...] = hidden.T.reshape(turned)
-    hnt_copy = send_one(hn_t.at[:, :, other], hn_p, core_peer)
-    first_of_down(3)
-    inner = act[0]
-    for s, n in tiles(D, 512):
-        xn[:, s : s + n] = dot(inner, wd[..., s : s + n].reshape(FC, n)).astype(BF16)
-    hnt_copy.wait_recv()
-    act_groups[1].wait_recv()
-    weight_grad(1, first_rows, hn_t, hn_p, act.at[1], act_p.at[1])
-    rs_send(1, 0)
+        piece = pl.ds(s, n)
+        act_groups[t].send(act.at[:, :, piece], act_p.at[:, :, piece], core_peer)
+        if t == 0:
+            ct_copy.wait_recv()
+            hnt_copy.wait_recv()
+        else:
+            first_of_tile(t - 1)
 
     for scatter in attn_sums:
         scatter.wait_send()
@@ -590,14 +587,15 @@
         r = dot_nt(act[1], wg[block].reshape(512, FC)) + dot_nt(act[2], wu[block].reshape(512, FC))
         zs[:, cols] = r.astype(BF16)
         dhn_sums[0].first((t * 512, None, 512) if t < 2 else (None, t * 512, 512))
-        if t == 2:
-            act_groups[2].wait_recv()
-            weight_grad(2, first_rows, hn_t, hn_p, act.at[2], act_p.at[2])
-            rs_send(2, 0)
+        if t == 0:
+            first_of_tile(3)
     dhn_sums[1].first()
+    inner = act[0]
+    for s, n in tiles(D, 512):
+        xn[:, s : s + n] = dot(inner, wd[..., s : s + n].reshape(FC, n)).astype(BF16)
     weight_grad(0, other_rows, c_t, c_p, act.at[0], act_p.at[0])
+    dhn_sums[0].second()
     rs_turn(0, 0)
-    dhn_sums[0].second()
     dhn_sums[1].second()
     weight_grad(1, other_rows, hn_t, hn_p, act.at[1], act_p.at[1])
     weight_grad(2, other_rows, hn_t, hn_p, act.at[2], act_p.at[2])
@@ -622,7 +620,7 @@
     rs_turn(1, 0)
     da_parts[0].second()
     da_parts[1].second()
-    rs_turn(2, 0)
+    rs_turn(2, 0, (1,))
     rs_turn(0, 1)
 
     for part in da_parts:
@@ -671,9 +669,14 @@
         for c, goal in ((0, core), (1, other)):
             if step != 0 or c == 1:
                 dkv_group.send(kvall.at[chip * 2 + goal], dkv_r.at[i, c], (iy, chip * 2 + goal, iz))
-        if i == 1:
-            for scatter in ffn_sums:
-                scatter.second()
+        if i == 2:
+            dat_copy.wait_recv()
+            ob_copy.wait_recv()
+            weight_grad(3, first_rows, c_t, da_p, ob, ob_p)
+            rs_send(3, 0)
+            rs_turn(2, 0, (0,))
+    for scatter in ffn_sums:
+        scatter.second()
     dq_t = dot(kt[...], pt[...]) * (HD ** -0.5)
     for p in range(PAIRS):
         a0 = dq_t[:, p * 256 : p * 256 + 128].T
@@ -685,16 +688,10 @@
         dqp[:, p * 128 : (p + 1) * 128] = rot_back(dq).astype(BF16)
     dqp_copy = send_one(dqp, dqp_p, core_peer)
 
-    bo_parts = []
-    for part in range(2):
-        bo_s[kept[part], :] = (mid[kept[part], :] + ffn_sums[part].result()).astype(BF16)
-        copy_local(bo_s.at[kept[part]], bo.at[z_rows(part, iz)])
-        bo_parts.append(ZGather(bo, part, bo_s))
-    dat_copy.wait_recv()
-    ob_copy.wait_recv()
-    weight_grad(3, first_rows, c_t, da_p, ob, ob_p)
-    rs_send(3, 0)
-    weight_grad(3, other_rows, c_t, da_p, ob, ob_p)
+    xnt_copy.wait_recv()
+    dqp_copy.wait_recv()
+    weight_grad(4, first_rows, xn_t, xn_p, dqp, dqp_p)
+    rs_send(4, 0)
     rs_turn(1, 1)
 
     dkv_group.wait_recv()
@@ -716,19 +713,23 @@
         dxn_sums[0].first((l, l + D // 2, 512))
     dxn_sums[1].first()
 
-    for part in bo_parts:
-        part.second()
-    xnt_copy.wait_recv()
-    dqp_copy.wait_recv()
-    weight_grad(4, first_rows, xn_t, xn_p, dqp, dqp_p, n=512)
     dkvp_copy.wait_recv()
-    weight_grad(4, first_rows, xn_t, xn_p, dkvp, dkvp_p, n=128, shift=512)
-    rs_send(4, 0)
+    weight_grad(5, first_rows, xn_t, xn_p, dkvp, dkvp_p)
+    rs_send(5, 0)
+    weight_grad(3, other_rows, c_t, da_p, ob, ob_p)
     dxn_sums[0].second()
     dxn_sums[1].second()
-    weight_grad(4, other_rows, xn_t, xn_p, dqp, dqp_p, n=512)
-    weight_grad(4, other_rows, xn_t, xn_p, dkvp, dkvp_p, n=128, shift=512)
+    bo_parts = []
+    for part in range(2):
+        bo_s[kept[part], :] = (mid[kept[part], :] + ffn_sums[part].result()).astype(BF16)
+        copy_local(bo_s.at[kept[part]], bo.at[z_rows(part, iz)])
+        bo_parts.append(ZGather(bo, part, bo_s))
+    weight_grad(4, other_rows, xn_t, xn_p, dqp, dqp_p)
+    weight_grad(5, other_rows, xn_t, xn_p, dkvp, dkvp_p)
     rs_turn(3, 0)
+    rs_turn(4, 0)
+    rs_turn(5, 0)
+    rs_turn(0, 2)
 
     gi_parts = []
 
@@ -744,19 +745,22 @@
         copy_local(gi_s.at[kept[part]], gi.at[z_rows(part, iz)])
         gi_parts.append(ZGather(gi, part, gi_s))
 
-    rs_turn(4, 0)
-    rs_turn(2, 1)
     first_norm_back(0)
     first_norm_back(1)
+    for part in bo_parts:
+        part.second()
+    rs_turn(2, 1)
     rs_turn(1, 2)
-    rs_turn(4, 1)
     gi_parts[0].second()
     gi_parts[1].second()
+    rs_turn(3, 1)
+    rs_turn(4, 1)
+    rs_turn(5, 1)
+    rs_last(0, [(g_d, o_d, 0, FC)])
     rs_turn(2, 2)
-    rs_turn(3, 1)
-    rs_turn(0, 2)
+    rs_last(1, [(g_g, o_g, 0, FC)])
     rs_turn(4, 2)
-    rs_last(1, [(g_g, o_g, 0, FC)])
+    rs_turn(5, 2)
     rs_turn(3, 2)
     rs_last(2, [(g_u, o_u, 0, FC)])
 
@@ -786,9 +790,9 @@
         return total[0:1]
 
     gain_f_group = exchange_gain(0, [(g_g, row_g), (g_u, row_u)])
-    rs_last(4, [(g_q, o_q, 0, 512), (g_kv, o_kv, 512, 128)])
+    rs_last(4, [(g_q, o_q, 0, 512)])
+    rs_last(5, [(g_kv, o_kv, 0, 128)])
     gain_a_group = exchange_gain(1, [(g_q, row_q), (g_kv, row_kv)])
-    rs_last(0, [(g_d, o_d, 0, FC)])
     rs_last(3, [(g_o, o_o, 0, 512)])
     chip_cols = pl.ds(pl.multiple_of((iy * 4 + ix) * 128, 128), 128)
 
@@ -837,8 +841,8 @@
         copy.wait()
 
 
-N_GROUPS = 76
-N_LOCAL = 32
+N_GROUPS = 95
+N_LOCAL = 26
 
 
 def per_device(
@@ -871,7 +875,7 @@
             ((R, D), F32), ((R, D), F32),
             ((T, D), BF16), ((T, D), BF16), ((R, D), BF16), ((R, D), BF16),
             ((T, FC), F32), ((3, T, FC), BF16), ((3, T, FC), BF16),
-            ((2, 4, 32, FC), BF16),
+            ((3, 2, 4, 32, FC), BF16),
             (turned, BF16), (turned, BF16), (turned, BF16),
             (half_turned, BF16), (half_turned, BF16), (half_turned, BF16), (half_turned, BF16),
             ((T, QC), BF16), ((T, QC), BF16), ((T, QC), BF16),
@@ -881,8 +885,6 @@
             ((3, 2, 2, 16, FC), BF16), ((3, 2, 2, 32, FC), BF16),
             ((2, 2, 2, 32, 1152), BF16), ((2, 2, 4, 32, 1152), BF16),
             ((2, 2, 16, 1152), BF16), ((2, 2, 32, 1152), BF16),
-            ((64, QC), F32), ((64, 128), F32), ((64, QC), F32),
-            ((64, FC), F32), ((64, FC), F32), ((64, FC), F32),
             ((2, 8, 64), F32), ((2, 3, 8, 64), F32),
         )
     ] + [

time: 119 us -> 115 us (0.966)
  Pallas kernels: 118 us -> 113 us
    pallas_call x1, Pallas kernels: 115 us -> 110 us  [per_device(): pl.pallas_call(layer_kernel, out_shape=(shape((T, D), BF16), shape((T, D)...]
where the time goes in v4:
time: 115 us; the launch traced here: 114 us
  Pallas kernels  113 us (98%)
    pallas_call x1, Pallas kernels, per_device(): pl.pallas_call(layer_kernel, out_shape=(shape((T, D), BF16), shape((T, D)...  110 us
    pallas_call x1, Pallas kernels, per_device(): pl.pallas_call(store_kernel, out_shape=(shape((T, D), BF16), shape((T, D)...  3.09 us

profile of v4, /device:TPU:0, one launch (start us, length us, event | category | flops | bytes accessed | tf_op | source)
XLA Modules:
  0.0 113.8 jit_solution(6621281682194624079)
XLA Ops:
  0.6 109.9 %shard_map.204 = (bf16[192,2048]{1,0:T(8,128)(2,1)}, bf16[192,2048]{1,0:T(8,128)(2,1)}, f32[64,512]{1,0:T(8,128)}, f32[64,128]{1,0:T(8,128)}, f32[64,512]{1,0:T(...) custom-call(s32[1,16]{1,0:T(1,128)} %order.1, ...), custom_call_target="tpu_custom_call" | custom-call | tf_op jit(solution)/shard_map/pallas_call | solution.py:900
  110.6 3.1 %shard_map.205 = (bf16[192,2048]{1,0:T(8,128)(2,1)}, f32[192,2048]{1,0:T(8,128)}, f32[64,512]{1,0:T(8,128)}, f32[64,128]{1,0:T(8,128)}, f32[64,512]{1,0:T(8,128)...) custom-call(bf16[192,2048]{1,0:T(8,128)(2,1)} %get-tuple-element.30.r, ...), custom_call_target="tpu_custom_call" | custom-call | tf_op jit(solution)/shard_map/pallas_call | solution.py:915

commit v5 on v4

--- a/solution.py
+++ b/solution.py
@@ -595,8 +595,8 @@
         xn[:, s : s + n] = dot(inner, wd[..., s : s + n].reshape(FC, n)).astype(BF16)
     weight_grad(0, other_rows, c_t, c_p, act.at[0], act_p.at[0])
     dhn_sums[0].second()
+    dhn_sums[1].second()
     rs_turn(0, 0)
-    dhn_sums[1].second()
     weight_grad(1, other_rows, hn_t, hn_p, act.at[1], act_p.at[1])
     weight_grad(2, other_rows, hn_t, hn_p, act.at[2], act_p.at[2])
 

time: 115 us -> 115 us (level)
  no operation moved by 1% of the time
where the time goes in v5:
time: 115 us; the launch traced here: 114 us
  Pallas kernels  114 us (99%)
    pallas_call x1, Pallas kernels, per_device(): pl.pallas_call(layer_kernel, out_shape=(shape((T, D), BF16), shape((T, D)...  110 us
    pallas_call x1, Pallas kernels, per_device(): pl.pallas_call(store_kernel, out_shape=(shape((T, D), BF16), shape((T, D)...  3.09 us

profile of v5, /device:TPU:0, one launch (start us, length us, event | category | flops | bytes accessed | tf_op | source)
XLA Modules:
  0.0 114.4 jit_solution(16122660651858744102)
XLA Ops:
  0.6 110.5 %shard_map.204 = (bf16[192,2048]{1,0:T(8,128)(2,1)}, bf16[192,2048]{1,0:T(8,128)(2,1)}, f32[64,512]{1,0:T(8,128)}, f32[64,128]{1,0:T(8,128)}, f32[64,512]{1,0:T(...) custom-call(s32[1,16]{1,0:T(1,128)} %order.1, ...), custom_call_target="tpu_custom_call" | custom-call | tf_op jit(solution)/shard_map/pallas_call | solution.py:900
  111.1 3.1 %shard_map.205 = (bf16[192,2048]{1,0:T(8,128)(2,1)}, f32[192,2048]{1,0:T(8,128)}, f32[64,512]{1,0:T(8,128)}, f32[64,128]{1,0:T(8,128)}, f32[64,512]{1,0:T(8,128)...) custom-call(bf16[192,2048]{1,0:T(8,128)(2,1)} %get-tuple-element.30.r, ...), custom_call_target="tpu_custom_call" | custom-call | tf_op jit(solution)/shard_map/pallas_call | solution.py:915
